TPU v7x, 128 devices: a whole 4x4x4 slice. The times are simulated.
128 devices in a mesh: dp: 32 (over y, x, core), tensor: 4 (over z).
Axes of the slice: x: 4, y: 4, z: 4, core: 2. Of those that a mesh axis runs over, the one named last changes fastest.
Arguments:
- out_grad: bfloat16 [65536, 2048], P('dp'), may hold values from -0.046875 to 0.046875
- inputs: bfloat16 [65536, 8192], P('dp', 'tensor'), may hold values from -6 to 6
- weights: float32 [2048, 8192], P('dp', 'tensor'), may hold values from -60 to 60
- moment: float32 [2048, 8192], P('dp', 'tensor'), may hold values from -3 to 3
- second: float32 [2048, 8192], P('dp', 'tensor'), may hold values from 0.05 to 2
Outputs:
- new_weights: float32 [2048, 8192], P('dp', 'tensor')
- new_moment: float32 [2048, 8192], P('dp', 'tensor')
- new_second: float32 [2048, 8192], P('dp', 'tensor')
All inputs are finite; a program needn't handle non-finite values.
Results may differ from a plain program's by a relative error of at most 0.0003.
Values sent between devices are 32-bit elements; how exact they have to be, the bound alone decides.
No kernel may reach another device: no remote copies, remote signals or barrier semaphores. Data moves between devices by JAX's collectives and lax.ppermute only.
A program may use at most 128 MiB of HBM per device.

v0:
```python
import jax
import jax.numpy as jnp
from jax import lax
from jax.sharding import PartitionSpec as P


def finish(grad, weights, moment, second):
    new_moment = 0.9 * moment + 0.1 * grad
    new_second = 0.95 * second + 0.05 * grad * grad
    step_size = 0.3 * (new_moment / (1.0 - 0.9**10))
    moved = weights - step_size / (jnp.sqrt(new_second / (1.0 - 0.95**10)) + 1e-08)
    return (moved, new_moment, new_second)


def rescale(moved, totals, width):
    mean_square = totals[:, None] / width
    return moved / jnp.sqrt(mean_square + 1e-06)


def on_device(out_grad, inputs, weights, moment, second):
    width = weights.shape[1] * lax.axis_size("tensor")
    grad = lax.psum_scatter(
        lax.dot_general(
            out_grad, inputs, (((0,), (0,)), ((), ())), preferred_element_type=jnp.float32
        ),
        "dp",
        scatter_dimension=0,
        tiled=True,
    )
    moved, new_moment, new_second = finish(grad, weights, moment, second)
    totals = lax.psum(jnp.sum(moved * moved, axis=1), "tensor")
    return (rescale(moved, totals, width), new_moment, new_second)


def solution(mesh):
    in_specs = (
        P("dp", None),
        P("dp", "tensor"),
        P("dp", "tensor"),
        P("dp", "tensor"),
        P("dp", "tensor"),
    )
    out_specs = (P("dp", "tensor"), P("dp", "tensor"), P("dp", "tensor"))
    return jax.shard_map(
        on_device, mesh=mesh, in_specs=in_specs, out_specs=out_specs, check_vma=False
    )
```

profile of v0, /device:TPU:0, one launch (start us, length us, event | category | flops | bytes accessed | tf_op | source)
XLA Modules:
  0.0 170.2 jit_solution(12142228534683295449)
XLA Ops:
  7.2 0.0 reduce-scatter.2.cloned.1.call-start
  7.2 24.3 %fusion.2 = f32[2048,2048]{1,0:T(8,128)} fusion(bf16[2048,2048]{1,0:T(8,128)(2,1)} %param.5, bf16[2048,2048]{1,0:T(8,128)(2,1)} %param.6), kind=kOutput, calls=%fused_computation.7 | convolution fusion | flops 17179869184 | bytes 33554432 | tf_op jit(solution)/shard_map/dot_general | solution.py:23
  31.5 0.0 copy-start
  31.5 0.0 copy-start.1
  31.5 0.0 copy-start.2
  31.5 0.0 reduce-scatter.2.cloned.1.call-update
  31.5 117.7 %reduce-scatter.2.cloned.1.call-done = f32[64,2048]{1,0:T(8,128)} async-done(((f32[2048,2048]{1,0:T(8,128)}), f32[64,2048]{1,0:T(8,128)}) %reduce-scatter.2.cloned.1.call-update) | async-done | bytes 524304 | tf_op jit(solution)/shard_map/reduce_scatter | solution.py:22
  149.2 0.0 copy-done
  149.2 0.0 copy-done.1
  149.2 0.0 copy-done.2
  149.2 2.5 %multiply_reduce_fusion = (f32[64]{0:T(128)S(1)}, f32[64,2048]{1,0:T(8,128)S(1)}, f32[64,2048]{1,0:T(8,128)}, f32[64,2048]{1,0:T(8,128)}) fusion(f32[64,2048]{1,0:T(8,128)S(1)} %copy-done, f32[64,2048]{1,0:T(8,128)} %reduce-scatter.2.cloned.1.call-done, f32[64,2048]{1,0:T(8,128)S(1)} %copy-done.1, f32[64,2048]{1,0:T(8,128)S(1)} %copy-done.2), kind=kLoop, calls=%fused_computation.2 | loop fusion | flops 1834944 | bytes 3670272 | tf_op jit(solution)/shard_map/reduce_sum | solution.py:31
  151.7 10.7 %psum.7 = f32[64]{0:T(128)S(1)} all-reduce(f32[64]{0:T(128)S(1)} %get-tuple-element.3), channel_id=1, replica_groups=mesh['dp'=32,'tensor'=4] {'tensor'}, use_global_device_ids=true, to_apply=%region_2.0 | all-reduce | flops 64 | bytes 512 | tf_op jit(solution)/shard_map/psum | solution.py:31
  162.4 0.9 broadcast_divide_fusion
  (1 shorter events, 0.0 us)
Async XLA Ops:
  7.2 142.1 %reduce-scatter.2.cloned.1.call-start = ((), (), s32[]{:S(2)}) async-start(), calls=%async_computation.1 | async-start | bytes 17301504 | tf_op jit(solution)/shard_map/reduce_scatter | solution.py:22
  31.5 117.7 %copy-start = (f32[64,2048]{1,0:T(8,128)S(1)}, f32[64,2048]{1,0:T(8,128)}, u32[]{:S(2)}) copy-start(f32[64,2048]{1,0:T(8,128)} %param.7) | copy-start | bytes 1572868
  31.5 117.7 %copy-start.1 = (f32[64,2048]{1,0:T(8,128)S(1)}, f32[64,2048]{1,0:T(8,128)}, u32[]{:S(2)}) copy-start(f32[64,2048]{1,0:T(8,128)} %param.8) | copy-start | bytes 1572868
  31.5 117.7 %copy-start.2 = (f32[64,2048]{1,0:T(8,128)S(1)}, f32[64,2048]{1,0:T(8,128)}, u32[]{:S(2)}) copy-start(f32[64,2048]{1,0:T(8,128)} %param.9) | copy-start | bytes 1572868
Sparse Core Ops, SparseCore 0:
  31.6 117.5 reduce-scatter.1
where the time goes:
time: 170 us
  waiting for transfers between devices  118 us (69%)
  matrix products  24.3 us (14%)
  between operations  14 us (8%)
  blocking collectives  10.7 us (6%)
  other arithmetic  3.39 us (2%)
    reduce_scatter x1, waiting for transfers between devices, on_device(): lax.psum_scatter(lax.dot_general(out_grad, inputs, (((0,), (0,)), ((), ()...  118 us
    dot_general x1, matrix products, on_device(): lax.dot_general(out_grad, inputs, (((0,), (0,)), ((), ())), preferred_ele...  24.3 us
    psum x1, blocking collectives, on_device(): totals = lax.psum(jnp.sum(moved * moved, axis=1), 'tensor')  10.7 us
  transfers between devices with their start and end apart: 1, of which 1 were waited for; matrix products, arithmetic and copies ran while one was open for 0% of the time, Pallas kernels for 0%

commit v1 on v0

v1 whole, which is shorter than its diff:
```python
import functools

import jax
import jax.numpy as jnp
from jax import lax
from jax.experimental import pallas as pl
from jax.experimental.pallas import tpu as pltpu
from jax.sharding import PartitionSpec as P

F32 = jnp.float32
BF16 = jnp.bfloat16
MIB = 2**20
VMEM = pltpu.VMEM
ROWS = 64
TILES = 16
CHAINS = ((0, 1024, (0, 1, 2, 3)), (1024, 1024, (1, 0, 3, 2)))

RING_A = (1, 0, 3, 2)
RING_B = (3, 2, 1, 0)


def device_index(y, x, core):
    return (y * 4 + x) * 2 + core


def swap_pairs(kind):
    partner = RING_B if kind % 2 else RING_A
    pairs = []
    for y in range(4):
        for x in range(4):
            for core in range(2):
                along_x = (core == 0) == (kind < 2)
                to = (y, partner[x]) if along_x else (partner[y], x)
                pairs.append((device_index(y, x, core), device_index(*to, core)))
    return pairs


SWAPS = [swap_pairs(kind) for kind in range(4)]
CORE_SWAP = [(i, i ^ 1) for i in range(32)]
Z_SWAPS = (list(enumerate(RING_A)), list(enumerate(RING_B)))


def params(mib, **more):
    return pltpu.CompilerParams(vmem_limit_bytes=mib * MIB, **more)


def in_vmem():
    return pl.BlockSpec(memory_space=VMEM)


def gray(i):
    high = lax.shift_right_logical(i, 1)
    return high ^ (i & 1), high


def prep_kernel(tiles, out_grad, turned):
    me = lax.axis_index("dp")
    core = me & 1
    my_x = gray(lax.shift_right_logical(me, 1) & 3)
    my_y = gray(lax.shift_right_logical(me, 3))
    for k in range(tiles):
        tile = pl.program_id(0) * tiles + k
        xa, xb = [a ^ b for a, b in zip(gray(tile & 3), my_x)]
        ya, yb = [a ^ b for a, b in zip(gray(lax.shift_right_logical(tile, 2)), my_y)]
        place0 = xa * 8 + xb * 4 + ya * 2 + yb + 16 * (1 - core)
        place1 = ya * 8 + yb * 4 + xa * 2 + xb + 16 * core
        block = out_grad[:, k * 128 : (k + 1) * 128].T
        turned[pl.ds(place0, 1)] = block[:ROWS][None]
        turned[pl.ds(place1, 1)] = block[ROWS:][None]


def prep(out_grad):
    tokens, rows = out_grad.shape
    tiles = 2
    return pl.pallas_call(
        functools.partial(prep_kernel, tiles),
        grid=(TILES // tiles,),
        out_shape=pltpu.VMEM((2 * TILES, ROWS, tokens), BF16),
        in_specs=[pl.BlockSpec((tokens, tiles * 128), lambda i: (0, i))],
        out_specs=in_vmem(),
        compiler_params=params(16),
        name="prep",
    )(out_grad)


def gemm_kernel(blocks, first, width, add, *refs):
    if add:
        turned, inputs, received, out = refs
    else:
        turned, inputs, out = refs
    row = 0
    for lo, hi in blocks:
        left = turned[lo:hi].reshape((hi - lo) * ROWS, turned.shape[2])
        for col in range(0, width, 256):
            part = jnp.dot(
                left, inputs[:, first + col : first + col + 256], preferred_element_type=F32
            )
            if add:
                part = part + received[row : row + (hi - lo) * ROWS, col : col + 256]
            out[row : row + (hi - lo) * ROWS, col : col + 256] = part
        row += (hi - lo) * ROWS


def gemm(name, turned, inputs, blocks, first, width, received=None):
    rows = sum(hi - lo for lo, hi in blocks) * ROWS
    tokens = inputs.shape[0]
    args = (turned, inputs) + (() if received is None else (received,))
    return pl.pallas_call(
        functools.partial(gemm_kernel, blocks, first, width, received is not None),
        out_shape=pltpu.VMEM((rows, width), F32),
        in_specs=[in_vmem()] * len(args),
        out_specs=in_vmem(),
        compiler_params=params(4),
        cost_estimate=pl.CostEstimate(
            flops=2 * rows * width * tokens, bytes_accessed=rows * width * 4, transcendentals=0
        ),
        name=name,
    )(*args)


def blocks_of(order, side, sent):
    base = 0 if side == "sib" else TILES
    if order[0] == 0:
        lo = base + 8 * sent
        return ((lo, lo + 8),)
    lo = base + 4 * sent
    return ((lo, lo + 4), (lo + 8, lo + 12))


def finish_kernel(kept, came, weights, moment, second, moved, new_moment, new_second, sums):
    total = jnp.zeros((ROWS, 128), F32)
    for (first, width, _), a, b in zip(CHAINS, kept, came):
        for col in range(0, width, 128):
            here = (slice(None), slice(first + col, first + col + 128))
            grad = a[:, col : col + 128] + b[:, col : col + 128]
            m = 0.9 * moment[here] + 0.1 * grad
            v = 0.95 * second[here] + 0.05 * grad * grad
            step = 0.3 * (m / (1.0 - 0.9**10))
            w = weights[here] - step / (jnp.sqrt(v / (1.0 - 0.95**10)) + 1e-08)
            new_moment[here] = m
            new_second[here] = v
            moved[here] = w
            total = total + w * w
    sums[...] = jnp.broadcast_to(jnp.sum(total, axis=1, keepdims=True), sums.shape)


def finish(kept, came, weights, moment, second):
    n = len(CHAINS)

    def kernel(*refs):
        finish_kernel(refs[:n], refs[n : 2 * n], *refs[2 * n :])

    shape = jax.ShapeDtypeStruct(weights.shape, F32)
    return pl.pallas_call(
        kernel,
        out_shape=(pltpu.VMEM(weights.shape, F32), shape, shape, pltpu.VMEM((ROWS, 128), F32)),
        in_specs=[in_vmem()] * (2 * n + 3),
        out_specs=[in_vmem()] * 4,
        compiler_params=params(8),
        name="finish",
    )(*kept, *came, weights, moment, second)


def rescale_kernel(width, moved, mine, theirs, out):
    scale = lax.rsqrt((mine[...] + theirs[...]) / width + 1e-06)
    for col in range(0, moved.shape[1], 128):
        out[:, col : col + 128] = moved[:, col : col + 128] * scale


def rescale(moved, mine, theirs, width):
    return pl.pallas_call(
        functools.partial(rescale_kernel, width),
        out_shape=jax.ShapeDtypeStruct(moved.shape, F32),
        in_specs=[in_vmem()] * 3,
        out_specs=in_vmem(),
        compiler_params=params(4),
        name="rescale",
    )(moved, mine, theirs)


def on_device(out_grad, inputs, weights, moment, second):
    width = weights.shape[1] * lax.axis_size("tensor")
    inputs = pltpu.with_memory_space_constraint(inputs, VMEM)
    turned = prep(out_grad)
    sent = []
    for i, (first, cols, order) in enumerate(CHAINS):
        part = gemm(f"sib_sent_{i}", turned, inputs, blocks_of(order, "sib", 1), first, cols)
        sent.append(lax.ppermute(part, "dp", CORE_SWAP))
    came = []
    for i, (first, cols, order) in enumerate(CHAINS):
        part = gemm(f"own_sent_{i}", turned, inputs, blocks_of(order, "own", 1), first, cols, sent[i])
        came.append(lax.ppermute(part, "dp", SWAPS[order[0]]))
    other = []
    for i, (first, cols, order) in enumerate(CHAINS):
        part = gemm(f"sib_kept_{i}", turned, inputs, blocks_of(order, "sib", 0), first, cols)
        other.append(lax.ppermute(part, "dp", CORE_SWAP))
    kept = []
    for i, (first, cols, order) in enumerate(CHAINS):
        kept.append(gemm(f"own_kept_{i}", turned, inputs, blocks_of(order, "own", 0), first, cols, other[i]))
    for step in range(1, 4):
        for i, (first, cols, order) in enumerate(CHAINS):
            size = kept[i].shape[0] // 2
            a, b = kept[i], came[i]
            if step == 2 and order[2] == 3:
                a, b = [z.reshape(2, 2, ROWS, cols) for z in (a, b)]
                up, down = [(a[:, k] + b[:, k]).reshape(size, cols) for k in (1, 0)]
            else:
                up, down = a[size:] + b[size:], a[:size] + b[:size]
            came[i] = lax.ppermute(up, "dp", SWAPS[order[step]])
            kept[i] = down
    moved, new_moment, new_second, sums = finish(kept, came, weights, moment, second)
    sums = sums + lax.ppermute(sums, "tensor", Z_SWAPS[0])
    theirs = lax.ppermute(sums, "tensor", Z_SWAPS[1])
    return rescale(moved, sums, theirs, width), new_moment, new_second


def solution(mesh):
    spec = P("dp", "tensor")
    return jax.shard_map(
        on_device,
        mesh=mesh,
        in_specs=(P("dp", None), spec, spec, spec, spec),
        out_specs=(spec, spec, spec),
        check_vma=False,
    )
```

time: 170 us -> 102 us (0.60)
  waiting for transfers between devices: 118 us -> 49.9 us
  Pallas kernels: 0 us -> 24.8 us
  matrix products: 24.3 us -> 0 us
  starting transfers between devices: 0.04 us -> 21.1 us
  between operations: 14 us -> 0.8 us
  blocking collectives: 10.7 us -> 0 us
  local copies, waits for them, and re-layouts: 0.01 us -> 3.4 us
  other arithmetic: 3.39 us -> 1.52 us
    reduce_scatter x1 -> x0, waiting for transfers between devices: 118 us -> none  [on_device(): lax.psum_scatter(lax.dot_general(out_grad, inputs, (((0,), (0,)), ((), ()...]
    ppermute x0 -> x14, waiting for transfers between devices: none -> 49.9 us  [the longest x6 25.8 us: on_device(): came[i] = lax.ppermute(up, 'dp', SWAPS[order[step]])]
    pallas_call x0 -> x11, Pallas kernels: none -> 24.8 us  [the longest x8 18.6 us: gemm(): pl.pallas_call(functools.partial(gemm_kernel, blocks, first, width, recei...]
    dot_general x1 -> x0, matrix products: 24.3 us -> none  [on_device(): lax.dot_general(out_grad, inputs, (((0,), (0,)), ((), ())), preferred_ele...]
    ppermute x0 -> x14, starting transfers between devices: none -> 21.1 us  [the longest x6 10.4 us: on_device(): came[i] = lax.ppermute(up, 'dp', SWAPS[order[step]])]
    psum x1 -> x0, blocking collectives: 10.7 us -> none  [on_device(): totals = lax.psum(jnp.sum(moved * moved, axis=1), 'tensor')]
    unnamed x6 -> x10, local copies, waits for them, and re-layouts: 0.01 us -> 3.4 us
    reduce_sum x1 -> x0, other arithmetic: 2.47 us -> none  [on_device(): totals = lax.psum(jnp.sum(moved * moved, axis=1), 'tensor')]
  transfers between devices with their start and end apart: 1 -> 14, of which waited for: 1 -> 8; matrix products, arithmetic and copies ran while one was open for 0% -> 1% of each run, Pallas kernels for 0% -> 16%
where the time goes in v1:
time: 102 us
  waiting for transfers between devices  49.9 us (49%)
  Pallas kernels  24.8 us (24%)
  starting transfers between devices  21.1 us (21%)
  local copies, waits for them, and re-layouts  3.4 us (3%)
  other arithmetic  1.52 us (1%)
    ppermute x6, waiting for transfers between devices, on_device(): came[i] = lax.ppermute(up, 'dp', SWAPS[order[step]])  25.8 us
    ppermute x2, waiting for transfers between devices, on_device(): came.append(lax.ppermute(part, 'dp', SWAPS[order[0]]))  20.1 us
    pallas_call x8, Pallas kernels, gemm(): pl.pallas_call(functools.partial(gemm_kernel, blocks, first, width, recei...  18.6 us
    ppermute x6, starting transfers between devices, on_device(): came[i] = lax.ppermute(up, 'dp', SWAPS[order[step]])  10.4 us
    ppermute x1, starting transfers between devices, on_device(): theirs = lax.ppermute(sums, 'tensor', Z_SWAPS[1])  4.04 us
    pallas_call x1, Pallas kernels, prep(): pl.pallas_call(functools.partial(prep_kernel, tiles), grid=(TILES // tile...  4.02 us
    ppermute x2, starting transfers between devices, on_device(): came.append(lax.ppermute(part, 'dp', SWAPS[order[0]]))  3.41 us
    unnamed x10, local copies, waits for them, and re-layouts  3.4 us
  transfers between devices with their start and end apart: 14, of which 8 were waited for; matrix products, arithmetic and copies ran while one was open for 1% of the time, Pallas kernels for 16%

profile of v1, /device:TPU:0, one launch (start us, length us, event | category | flops | bytes accessed | tf_op | source)
XLA Modules:
  0.0 101.5 jit_solution(7947165965048059466)
XLA Ops:
  0.6 3.4 %copy-done.1 = bf16[2048,2048]{1,0:T(8,128)(2,1)S(1)} copy-done((bf16[2048,2048]{1,0:T(8,128)(2,1)S(1)}, bf16[2048,2048]{1,0:T(8,128)(2,1)}, u32[]{:S(2)}) %copy-start.1) | copy-done | bytes 8388632
  4.0 4.0 %prep.1.refs_0_ = bf16[32,64,2048]{2,1,0:T(8,128)(2,1)S(1)} custom-call(bf16[2048,2048]{1,0:T(8,128)(2,1)S(1)} %copy-done.1), custom_call_target="tpu_custom_call" | custom-call | tf_op jit(solution)/shard_map/prep/pallas_call | solution.py:75
  8.1 2.3 %sib_sent_1.1 = f32[512,1024]{1,0:T(8,128)S(1)} custom-call(bf16[32,64,2048]{2,1,0:T(8,128)(2,1)S(1)} %prep.1.refs_0_, bf16[2048,2048]{1,0:T(8,128)(2,1)S(1)} %copy-done), custom_call_target="tpu_custom_call" | custom-call | flops 2147483648 | bytes 2097152 | tf_op jit(solution)/shard_map/sib_sent_1/pallas_call | solution.py:108
  10.5 2.3 %sib_sent_0.1 = f32[512,1024]{1,0:T(8,128)S(1)} custom-call(bf16[32,64,2048]{2,1,0:T(8,128)(2,1)S(1)} %prep.1.refs_0_, bf16[2048,2048]{1,0:T(8,128)(2,1)S(1)} %copy-done), custom_call_target="tpu_custom_call" | custom-call | flops 2147483648 | bytes 2097152 | tf_op jit(solution)/shard_map/sib_sent_0/pallas_call | solution.py:108
  13.4 2.3 %sib_kept_1.1 = f32[512,1024]{1,0:T(8,128)S(1)} custom-call(bf16[32,64,2048]{2,1,0:T(8,128)(2,1)S(1)} %prep.1.refs_0_, bf16[2048,2048]{1,0:T(8,128)(2,1)S(1)} %copy-done), custom_call_target="tpu_custom_call" | custom-call | flops 2147483648 | bytes 2097152 | tf_op jit(solution)/shard_map/sib_kept_1/pallas_call | solution.py:108
  15.8 2.3 %sib_kept_0.1 = f32[512,1024]{1,0:T(8,128)S(1)} custom-call(bf16[32,64,2048]{2,1,0:T(8,128)(2,1)S(1)} %prep.1.refs_0_, bf16[2048,2048]{1,0:T(8,128)(2,1)S(1)} %copy-done), custom_call_target="tpu_custom_call" | custom-call | flops 2147483648 | bytes 2097152 | tf_op jit(solution)/shard_map/sib_kept_0/pallas_call | solution.py:108
  18.7 2.3 %own_sent_1.1 = f32[512,1024]{1,0:T(8,128)S(1)} custom-call(bf16[32,64,2048]{2,1,0:T(8,128)(2,1)S(1)} %prep.1.refs_0_, bf16[2048,2048]{1,0:T(8,128)(2,1)S(1)} %copy-done, f32[512,1024]{1,0:T(8,128)S(1)} %collective-permute-done.6.refs_2_), custom_call_target="tpu_custom_call" | custom-call | flops 2147483648 | bytes 2097152 | tf_op jit(solution)/shard_map/own_sent_1/pallas_call | solution.py:108
  21.0 2.9 %collective-permute-start.7 = (f32[512,1024]{1,0:T(8,128)S(1)}, f32[512,1024]{1,0:T(8,128)S(1)}, u32[]{:S(2)}, u32[]{:S(2)}) collective-permute-start(f32[512,1024]{1,0:T(8,128)S(1)} %own_sent_1.1), channel_id=1, source_target_pairs={{0,24},{4,100},{8,16},{12,108},{16,8},{20,116},{24,0},{28,124},{32... | collective-permute-start | bytes 6291464 | tf_op jit(solution)/shard_map/ppermute | solution.py:192
  24.0 2.3 %own_sent_0.1 = f32[512,1024]{1,0:T(8,128)S(1)} custom-call(bf16[32,64,2048]{2,1,0:T(8,128)(2,1)S(1)} %prep.1.refs_0_, bf16[2048,2048]{1,0:T(8,128)(2,1)S(1)} %copy-done, f32[512,1024]{1,0:T(8,128)S(1)} %collective-permute-done.1.refs_2_), custom_call_target="tpu_custom_call" | custom-call | flops 2147483648 | bytes 2097152 | tf_op jit(solution)/shard_map/own_sent_0/pallas_call | solution.py:108
  26.8 2.3 %own_kept_1.1 = f32[512,1024]{1,0:T(8,128)S(1)} custom-call(bf16[32,64,2048]{2,1,0:T(8,128)(2,1)S(1)} %prep.1.refs_0_, bf16[2048,2048]{1,0:T(8,128)(2,1)S(1)} %copy-done, f32[512,1024]{1,0:T(8,128)S(1)} %collective-permute-done.5.refs_2_), custom_call_target="tpu_custom_call" | custom-call | flops 2147483648 | bytes 2097152 | tf_op jit(solution)/shard_map/own_kept_1/pallas_call | solution.py:108
  29.1 2.3 %own_kept_0.1 = f32[512,1024]{1,0:T(8,128)S(1)} custom-call(bf16[32,64,2048]{2,1,0:T(8,128)(2,1)S(1)} %prep.1.refs_0_, bf16[2048,2048]{1,0:T(8,128)(2,1)S(1)} %copy-done, f32[512,1024]{1,0:T(8,128)S(1)} %collective-permute-done.refs_2_), custom_call_target="tpu_custom_call" | custom-call | flops 2147483648 | bytes 2097152 | tf_op jit(solution)/shard_map/own_kept_0/pallas_call | solution.py:108
  31.5 16.9 %collective-permute-done.7 = f32[512,1024]{1,0:T(8,128)S(1)} collective-permute-done((f32[512,1024]{1,0:T(8,128)S(1)}, f32[512,1024]{1,0:T(8,128)S(1)}, u32[]{:S(2)}, u32[]{:S(2)}) %collective-permute-start.7) | collective-permute-done | bytes 2097184 | tf_op jit(solution)/shard_map/ppermute | solution.py:192
  49.4 3.2 %collective-permute-done.2 = f32[512,1024]{1,0:T(8,128)S(1)} collective-permute-done((f32[512,1024]{1,0:T(8,128)S(1)}, f32[512,1024]{1,0:T(8,128)S(1)}, u32[]{:S(2)}, u32[]{:S(2)}) %collective-permute-start.2) | collective-permute-done | bytes 2097184 | tf_op jit(solution)/shard_map/ppermute | solution.py:192
  53.6 10.2 %collective-permute-done.8 = f32[256,1024]{1,0:T(8,128)S(1)} collective-permute-done((f32[256,1024]{1,0:T(8,128)S(1)}, f32[256,1024]{1,0:T(8,128)S(1)}, u32[]{:S(2)}, u32[]{:S(2)}) %collective-permute-start.8) | collective-permute-done | bytes 1048608 | tf_op jit(solution)/shard_map/ppermute | solution.py:209
  64.0 3.1 %collective-permute-start.9 = (f32[128,1024]{1,0:T(8,128)S(1)}, f32[128,1024]{1,0:T(8,128)S(1)}, u32[]{:S(2)}, u32[]{:S(2)}) collective-permute-start(f32[128,1024]{1,0:T(8,128)S(1)} %bitcast.13), channel_id=1, source_target_pairs={{0,96},{4,28},{8,104},{12,20},{16,112},{20,12},{24,120},{28,4},{32... | collective-permute-start | bytes 1572872 | tf_op jit(solution)/shard_map/ppermute | solution.py:209
  67.1 4.3 %collective-permute-done.3 = f32[256,1024]{1,0:T(8,128)S(1)} collective-permute-done((f32[256,1024]{1,0:T(8,128)S(1)}, f32[256,1024]{1,0:T(8,128)S(1)}, u32[]{:S(2)}, u32[]{:S(2)}) %collective-permute-start.3) | collective-permute-done | bytes 1048608 | tf_op jit(solution)/shard_map/ppermute | solution.py:209
  71.6 2.9 %collective-permute-start.4 = (f32[128,1024]{1,0:T(8,128)S(1)}, f32[128,1024]{1,0:T(8,128)S(1)}, u32[]{:S(2)}, u32[]{:S(2)}) collective-permute-start(f32[128,1024]{1,0:T(8,128)S(1)} %get-tuple-element.18), channel_id=1, source_target_pairs={{0,32},{4,12},{8,40},{12,4},{16,48},{20,28},{24,56},{28,20},{32,0}... | collective-permute-start | bytes 1572872 | tf_op jit(solution)/shard_map/ppermute | solution.py:209
  75.0 6.7 %collective-permute-done.4 = f32[128,1024]{1,0:T(8,128)S(1)} collective-permute-done((f32[128,1024]{1,0:T(8,128)S(1)}, f32[128,1024]{1,0:T(8,128)S(1)}, u32[]{:S(2)}, u32[]{:S(2)}) %collective-permute-start.4) | collective-permute-done | bytes 524320 | tf_op jit(solution)/shard_map/ppermute | solution.py:209
  81.8 3.0 %collective-permute-start.10 = (f32[64,1024]{1,0:T(8,128)S(1)}, f32[64,1024]{1,0:T(8,128)S(1)}, u32[]{:S(2)}, u32[]{:S(2)}) collective-permute-start(f32[64,1024]{1,0:T(8,128)S(1)} %get-tuple-element.21), channel_id=1, source_target_pairs={{0,96},{4,28},{8,104},{12,20},{16,112},{20,12},{24,120},{28,4},{32... | collective-permute-start | bytes 786440 | tf_op jit(solution)/shard_map/ppermute | solution.py:209
  84.8 4.6 %collective-permute-done.10.refs_2_ = f32[64,1024]{1,0:T(8,128)S(1)} collective-permute-done((f32[64,1024]{1,0:T(8,128)S(1)}, f32[64,1024]{1,0:T(8,128)S(1)}, u32[]{:S(2)}, u32[]{:S(2)}) %collective-permute-start.10) | collective-permute-done | bytes 262176 | tf_op jit(solution)/shard_map/ppermute | solution.py:209
  90.8 1.9 %collective-permute-start.12 = (f32[64,128]{1,0:T(8,128)S(1)}, f32[64,128]{1,0:T(8,128)S(1)}, u32[]{:S(2)}, u32[]{:S(2)}) collective-permute-start(f32[64,128]{1,0:T(8,128)S(1)} %get-tuple-element.8), channel_id=1, source_target_pairs={{0,1},{1,0},{2,3},{3,2},{4,5},{5,4},{6,7},{7,6},{8,9},{9,8},{10,11... | collective-permute-start | bytes 98312 | tf_op jit(solution)/shard_map/ppermute | solution.py:212
  92.8 2.0 %collective-permute-done.12 = f32[64,128]{1,0:T(8,128)S(1)} collective-permute-done((f32[64,128]{1,0:T(8,128)S(1)}, f32[64,128]{1,0:T(8,128)S(1)}, u32[]{:S(2)}, u32[]{:S(2)}) %collective-permute-start.12) | collective-permute-done | bytes 32800 | tf_op jit(solution)/shard_map/ppermute | solution.py:212
  94.8 4.0 %collective-permute-start.13 = (f32[64,128]{1,0:T(8,128)S(1)}, f32[64,128]{1,0:T(8,128)S(1)}, u32[]{:S(2)}, u32[]{:S(2)}) collective-permute-start(f32[64,128]{1,0:T(8,128)S(1)} %add.57.mine), channel_id=1, source_target_pairs={{0,3},{1,2},{2,1},{3,0},{4,7},{5,6},{6,5},{7,4},{8,11},{9,10},{10,... | collective-permute-start | bytes 98312 | tf_op jit(solution)/shard_map/ppermute | solution.py:213
  98.8 1.9 %collective-permute-done.13.theirs = f32[64,128]{1,0:T(8,128)S(1)} collective-permute-done((f32[64,128]{1,0:T(8,128)S(1)}, f32[64,128]{1,0:T(8,128)S(1)}, u32[]{:S(2)}, u32[]{:S(2)}) %collective-permute-start.13) | collective-permute-done | bytes 32800 | tf_op jit(solution)/shard_map/ppermute | solution.py:213
  (32 shorter events, 6.9 us)
Async XLA Ops:
  0.6 3.4 %copy-start.1 = (bf16[2048,2048]{1,0:T(8,128)(2,1)S(1)}, bf16[2048,2048]{1,0:T(8,128)(2,1)}, u32[]{:S(2)}) copy-start(bf16[2048,2048]{1,0:T(8,128)(2,1)} %out_grad.1) | copy-start | bytes 25165828
  4.0 4.0 %copy-start = (bf16[2048,2048]{1,0:T(8,128)(2,1)S(1)}, bf16[2048,2048]{1,0:T(8,128)(2,1)}, u32[]{:S(2)}) copy-start(bf16[2048,2048]{1,0:T(8,128)(2,1)} %refs_1_.15) | copy-start | bytes 25165828
  10.4 8.3 %collective-permute-start.6 = (f32[512,1024]{1,0:T(8,128)S(1)}, f32[512,1024]{1,0:T(8,128)S(1)}, u32[]{:S(2)}, u32[]{:S(2)}) collective-permute-start(f32[512,1024]{1,0:T(8,128)S(1)} %sib_sent_1.1), channel_id=1, source_target_pairs={{0,4},{4,0},{8,12},{12,8},{16,20},{20,16},{24,28},{28,24},{32,36},... | collective-permute-start | bytes 6291464 | tf_op jit(solution)/shard_map/ppermute | solution.py:188
  12.8 11.2 %collective-permute-start.1 = (f32[512,1024]{1,0:T(8,128)S(1)}, f32[512,1024]{1,0:T(8,128)S(1)}, u32[]{:S(2)}, u32[]{:S(2)}) collective-permute-start(f32[512,1024]{1,0:T(8,128)S(1)} %sib_sent_0.1), channel_id=1, source_target_pairs={{0,4},{4,0},{8,12},{12,8},{16,20},{20,16},{24,28},{28,24},{32,36},... | collective-permute-start | bytes 6291464 | tf_op jit(solution)/shard_map/ppermute | solution.py:188
  15.7 11.1 %collective-permute-start.5 = (f32[512,1024]{1,0:T(8,128)S(1)}, f32[512,1024]{1,0:T(8,128)S(1)}, u32[]{:S(2)}, u32[]{:S(2)}) collective-permute-start(f32[512,1024]{1,0:T(8,128)S(1)} %sib_kept_1.1), channel_id=1, source_target_pairs={{0,4},{4,0},{8,12},{12,8},{16,20},{20,16},{24,28},{28,24},{32,36},... | collective-permute-start | bytes 6291464 | tf_op jit(solution)/shard_map/ppermute | solution.py:196
  18.1 11.0 %collective-permute-start = (f32[512,1024]{1,0:T(8,128)S(1)}, f32[512,1024]{1,0:T(8,128)S(1)}, u32[]{:S(2)}, u32[]{:S(2)}) collective-permute-start(f32[512,1024]{1,0:T(8,128)S(1)} %sib_kept_0.1), channel_id=1, source_target_pairs={{0,4},{4,0},{8,12},{12,8},{16,20},{20,16},{24,28},{28,24},{32,36},... | collective-permute-start | bytes 6291464 | tf_op jit(solution)/shard_map/ppermute | solution.py:196
  21.0 27.3 %collective-permute-start.7 = (f32[512,1024]{1,0:T(8,128)S(1)}, f32[512,1024]{1,0:T(8,128)S(1)}, u32[]{:S(2)}, u32[]{:S(2)}) collective-permute-start(f32[512,1024]{1,0:T(8,128)S(1)} %own_sent_1.1), channel_id=1, source_target_pairs={{0,24},{4,100},{8,16},{12,108},{16,8},{20,116},{24,0},{28,124},{32... | collective-permute-start | bytes 6291464 | tf_op jit(solution)/shard_map/ppermute | solution.py:192
  26.3 26.3 %collective-permute-start.2 = (f32[512,1024]{1,0:T(8,128)S(1)}, f32[512,1024]{1,0:T(8,128)S(1)}, u32[]{:S(2)}, u32[]{:S(2)}) collective-permute-start(f32[512,1024]{1,0:T(8,128)S(1)} %own_sent_0.1), channel_id=1, source_target_pairs={{0,8},{4,36},{8,0},{12,44},{16,24},{20,52},{24,16},{28,60},{32,40}... | collective-permute-start | bytes 6291464 | tf_op jit(solution)/shard_map/ppermute | solution.py:192
  48.9 14.9 %collective-permute-start.8 = (f32[256,1024]{1,0:T(8,128)S(1)}, f32[256,1024]{1,0:T(8,128)S(1)}, u32[]{:S(2)}, u32[]{:S(2)}) collective-permute-start(f32[256,1024]{1,0:T(8,128)S(1)} %get-tuple-element.12), channel_id=1, source_target_pairs={{0,8},{4,36},{8,0},{12,44},{16,24},{20,52},{24,16},{28,60},{32,40}... | collective-permute-start | bytes 3145736 | tf_op jit(solution)/shard_map/ppermute | solution.py:209
  53.2 18.3 %collective-permute-start.3 = (f32[256,1024]{1,0:T(8,128)S(1)}, f32[256,1024]{1,0:T(8,128)S(1)}, u32[]{:S(2)}, u32[]{:S(2)}) collective-permute-start(f32[256,1024]{1,0:T(8,128)S(1)} %get-tuple-element.14), channel_id=1, source_target_pairs={{0,24},{4,100},{8,16},{12,108},{16,8},{20,116},{24,0},{28,124},{32... | collective-permute-start | bytes 3145736 | tf_op jit(solution)/shard_map/ppermute | solution.py:209
  64.0 10.6 %collective-permute-start.9 = (f32[128,1024]{1,0:T(8,128)S(1)}, f32[128,1024]{1,0:T(8,128)S(1)}, u32[]{:S(2)}, u32[]{:S(2)}) collective-permute-start(f32[128,1024]{1,0:T(8,128)S(1)} %bitcast.13), channel_id=1, source_target_pairs={{0,96},{4,28},{8,104},{12,20},{16,112},{20,12},{24,120},{28,4},{32... | collective-permute-start | bytes 1572872 | tf_op jit(solution)/shard_map/ppermute | solution.py:209
  71.6 17.9 %copy-start.2 = (f32[64,2048]{1,0:T(8,128)S(1)}, f32[64,2048]{1,0:T(8,128)}, u32[]{:S(2)}) copy-start(f32[64,2048]{1,0:T(8,128)} %refs_4_.1) | copy-start | bytes 1572868
  71.6 17.9 %copy-start.3 = (f32[64,2048]{1,0:T(8,128)S(1)}, f32[64,2048]{1,0:T(8,128)}, u32[]{:S(2)}) copy-start(f32[64,2048]{1,0:T(8,128)} %refs_5_.1) | copy-start | bytes 1572868
  71.6 17.9 %copy-start.4 = (f32[64,2048]{1,0:T(8,128)S(1)}, f32[64,2048]{1,0:T(8,128)}, u32[]{:S(2)}) copy-start(f32[64,2048]{1,0:T(8,128)} %refs_6_.1) | copy-start | bytes 1572868
  71.6 10.1 %collective-permute-start.4 = (f32[128,1024]{1,0:T(8,128)S(1)}, f32[128,1024]{1,0:T(8,128)S(1)}, u32[]{:S(2)}, u32[]{:S(2)}) collective-permute-start(f32[128,1024]{1,0:T(8,128)S(1)} %get-tuple-element.18), channel_id=1, source_target_pairs={{0,32},{4,12},{8,40},{12,4},{16,48},{20,28},{24,56},{28,20},{32,0}... | collective-permute-start | bytes 1572872 | tf_op jit(solution)/shard_map/ppermute | solution.py:209
  74.6 10.2 %collective-permute-start.11 = (f32[64,1024]{1,0:T(8,128)S(1)}, f32[64,1024]{1,0:T(8,128)S(1)}, u32[]{:S(2)}, u32[]{:S(2)}) collective-permute-start(f32[64,1024]{1,0:T(8,128)S(1)} %get-tuple-element.19), channel_id=1, source_target_pairs={{0,32},{4,12},{8,40},{12,4},{16,48},{20,28},{24,56},{28,20},{32,0}... | collective-permute-start | bytes 786440 | tf_op jit(solution)/shard_map/ppermute | solution.py:209
  81.8 7.7 %collective-permute-start.10 = (f32[64,1024]{1,0:T(8,128)S(1)}, f32[64,1024]{1,0:T(8,128)S(1)}, u32[]{:S(2)}, u32[]{:S(2)}) collective-permute-start(f32[64,1024]{1,0:T(8,128)S(1)} %get-tuple-element.21), channel_id=1, source_target_pairs={{0,96},{4,28},{8,104},{12,20},{16,112},{20,12},{24,120},{28,4},{32... | collective-permute-start | bytes 786440 | tf_op jit(solution)/shard_map/ppermute | solution.py:209
  90.8 3.9 %collective-permute-start.12 = (f32[64,128]{1,0:T(8,128)S(1)}, f32[64,128]{1,0:T(8,128)S(1)}, u32[]{:S(2)}, u32[]{:S(2)}) collective-permute-start(f32[64,128]{1,0:T(8,128)S(1)} %get-tuple-element.8), channel_id=1, source_target_pairs={{0,1},{1,0},{2,3},{3,2},{4,5},{5,4},{6,7},{7,6},{8,9},{9,8},{10,11... | collective-permute-start | bytes 98312 | tf_op jit(solution)/shard_map/ppermute | solution.py:212
  94.8 5.9 %collective-permute-start.13 = (f32[64,128]{1,0:T(8,128)S(1)}, f32[64,128]{1,0:T(8,128)S(1)}, u32[]{:S(2)}, u32[]{:S(2)}) collective-permute-start(f32[64,128]{1,0:T(8,128)S(1)} %add.57.mine), channel_id=1, source_target_pairs={{0,3},{1,2},{2,1},{3,0},{4,7},{5,6},{6,5},{7,4},{8,11},{9,10},{10,... | collective-permute-start | bytes 98312 | tf_op jit(solution)/shard_map/ppermute | solution.py:213

commit v2 on v0

v2 whole, which is shorter than its diff:
```python
import functools

import jax
import jax.numpy as jnp
from jax import lax
from jax.experimental import pallas as pl
from jax.experimental.pallas import tpu as pltpu
from jax.sharding import PartitionSpec as P

F32 = jnp.float32
BF16 = jnp.bfloat16
MIB = 2**20
VMEM = pltpu.VMEM
ROWS = 64
TILES = 16
STRIPS = 8
FORTH, BACK = (0, 1, 2, 3), (1, 0, 3, 2)
CHAINS = ((0, 0, 768, FORTH), (1, 0, 768, BACK), (0, 768, 256, FORTH), (1, 768, 256, BACK))
ORDER = (
    "s1:0", "s1:1", "o1:0", "o1:1", "s0:01", "s1:23", "op:0", "op:1",
    "o1:2", "o1:3", "s0:23", "x2:0", "x2:1", "c2:0", "c2:1", "o0:2",
    "o0:3", "c2:2", "c2:3", "c3:02", "c3:13", "c4:0", "c4:1", "f:0",
    "f:1",
)
COSTS = {"x2:1": 20000000000, "c2:1": 10000000000, "f:0": 1000000000}

RING_A = (1, 0, 3, 2)
RING_B = (3, 2, 1, 0)


def device_index(y, x, core):
    return (y * 4 + x) * 2 + core


def swap_pairs(kind):
    partner = RING_B if kind % 2 else RING_A
    pairs = []
    for y in range(4):
        for x in range(4):
            for core in range(2):
                along_x = (core == 0) == (kind < 2)
                to = (y, partner[x]) if along_x else (partner[y], x)
                pairs.append((device_index(y, x, core), device_index(*to, core)))
    return pairs


SWAPS = [swap_pairs(kind) for kind in range(4)]
CORE_SWAP = [(i, i ^ 1) for i in range(32)]
Z_SWAPS = [list(enumerate(ring)) for ring in (RING_A, RING_B, (2, 3, 0, 1))]


def params(mib, **more):
    return pltpu.CompilerParams(vmem_limit_bytes=mib * MIB, **more)


def in_vmem():
    return pl.BlockSpec(memory_space=VMEM)


def gray(i):
    high = i >> 1
    return high ^ (i & 1), high


def half_copies(inputs, half, which, arrived, first):
    rows, width = half.shape[0] // STRIPS, half.shape[1]
    return [
        pltpu.make_async_copy(
            inputs.at[k * rows : (k + 1) * rows, which * width : (which + 1) * width],
            half.at[k * rows : (k + 1) * rows],
            arrived.at[first + k],
        )
        for k in range(STRIPS)
    ]


def prep_kernel(pieces, out_grad, inputs, turned, left, right, product, held, arrived):
    strips = held.shape[0]
    tiles = TILES // strips
    width = tiles * 128
    copies = [
        pltpu.make_async_copy(
            out_grad.at[:, k * width : (k + 1) * width], held.at[k], arrived.at[k]
        )
        for k in range(strips)
    ]
    copies += half_copies(inputs, left, 0, arrived, strips)
    copies += half_copies(inputs, right, 1, arrived, strips + STRIPS)
    for copy in copies:
        copy.start()
    me = lax.axis_index("dp")
    core = me & 1
    my_x = gray((me >> 1) & 3)
    my_y = gray(me >> 3)
    for tile in range(TILES):
        if tile % tiles == 0:
            copies[tile // tiles].wait()
        xa, xb = [a ^ b for a, b in zip(gray(tile & 3), my_x)]
        ya, yb = [a ^ b for a, b in zip(gray(tile >> 2), my_y)]
        place0 = xa * 8 + xb * 4 + ya * 2 + yb + 16 * (1 - core)
        place1 = ya * 8 + yb * 4 + xa * 2 + xb + 16 * core
        col = tile % tiles * 128
        block = held[tile // tiles, :, col : col + 128].T
        turned[pl.ds(place0, 1)] = block[:ROWS][None]
        turned[pl.ds(place1, 1)] = block[ROWS:][None]
    for copy in copies[strips : strips + STRIPS]:
        copy.wait()
    gemm_kernel(pieces, 0, 0, turned, left, right, product)
    for copy in copies[strips + STRIPS :]:
        copy.wait()


def prep(out_grad, inputs, pieces):
    tokens, rows = out_grad.shape
    strips = 8
    half = VMEM((tokens, inputs.shape[1] // 2), BF16)
    product = sum(hi - lo for (lo, hi), *_ in pieces) * ROWS, pieces[0][3]
    return pl.pallas_call(
        functools.partial(prep_kernel, pieces),
        out_shape=(VMEM((2 * TILES, ROWS, tokens), BF16), half, half, VMEM(product, F32)),
        in_specs=[pl.BlockSpec(memory_space=pl.ANY)] * 2,
        out_specs=[in_vmem()] * 4,
        scratch_shapes=[
            VMEM((strips, tokens, rows // strips), BF16),
            pltpu.SemaphoreType.DMA((strips + 2 * STRIPS,)),
        ],
        compiler_params=params(12),
        name="prep",
    )(out_grad, inputs)


def call(kernel, args, after, flops, **more):
    extra = () if after is None else (after,)

    def run(*refs):
        kernel(*refs[: len(args)], *refs[len(args) + len(extra) :])

    specs = [in_vmem()] * len(args) + [pl.BlockSpec(memory_space=pl.ANY)] * len(extra)
    cost = pl.CostEstimate(flops=flops, bytes_accessed=1, transcendentals=0)
    return pl.pallas_call(run, in_specs=specs, cost_estimate=cost, **more)(*args, *extra)


def gemm_kernel(pieces, offset, count, turned, *refs):
    halves, received, outs = refs[:2], refs[2 : 2 + count], refs[2 + count :]
    row = 0
    for (lo, hi), half, first, width in pieces:
        rows = (hi - lo) * ROWS
        left = turned[lo:hi].reshape(rows, turned.shape[2])
        out, at = outs[row // outs[0].shape[0]], row % outs[0].shape[0]
        for col in range(0, width, 256):
            right = halves[half][:, first + col : first + col + 256]
            part = jnp.dot(left, right, preferred_element_type=F32)
            if received:
                from_row = offset + row
                ref, come = received[from_row // received[0].shape[0]], from_row % received[0].shape[0]
                part = part + ref[come : come + rows, col : col + 256]
            out[at : at + rows, col : col + 256] = part
        row += rows


def gemm(name, after, cost, turned, halves, pieces, shares=1, received=(), offset=0):
    rows = sum(hi - lo for (lo, hi), *_ in pieces) * ROWS
    return call(
        functools.partial(gemm_kernel, pieces, offset, len(received)),
        (turned, *halves, *received),
        after,
        cost,
        out_shape=[VMEM((rows // shares, pieces[0][3]), F32)] * shares,
        out_specs=[in_vmem()] * shares,
        compiler_params=params(4),
        name=name,
    )


def pieces_of(chain, side, sent):
    *columns, order = CHAINS[chain]
    base = 0 if side == "s" else TILES
    if order[0] == 0:
        spans = ((base + 8 * sent, base + 8 * sent + 8),)
    else:
        spans = tuple((lo, lo + 4) for lo in (base + 4 * sent, base + 4 * sent + 8))
    return [(span, *columns) for span in spans]


def quarters(pieces):
    return [((at, at + 4), *columns) for (lo, hi), *columns in pieces for at in range(lo, hi, 4)]


def add_kernel(a, b, out):
    out[...] = a[...] + b[...]


def add(name, after, cost, a, b):
    return call(
        add_kernel,
        (a, b),
        after,
        cost,
        out_shape=VMEM(a.shape, F32),
        out_specs=in_vmem(),
        compiler_params=params(4),
        name=name,
    )


def combine_kernel(split, offset, *refs):
    *pairs, up, down = refs
    col = 0
    for kept, came in zip(pairs[::2], pairs[1::2]):
        rows, width = kept.shape
        size = rows // (2 * split)
        for i in range(split):
            for half, out in ((0, down), (1, up)):
                lo = (2 * i + half) * size
                out[i * size : (i + 1) * size, col : col + width] = (
                    kept[lo : lo + size] + came[offset + lo : offset + lo + size]
                )
        col += width


def combine(name, after, cost, split, pairs, offset=0):
    half = VMEM((pairs[0][0].shape[0] // 2, sum(kept.shape[1] for kept, _ in pairs)), F32)
    return call(
        functools.partial(combine_kernel, split, offset),
        [array for pair in pairs for array in pair],
        after,
        cost,
        out_shape=(half, half),
        out_specs=[in_vmem()] * 2,
        compiler_params=params(4),
        name=name,
    )


def finish_kernel(first, kept, came, weights, moment, second, *outs):
    moved, new_moment, new_second, sums = outs
    total = jnp.zeros((ROWS, 128), F32)
    for col in range(0, kept.shape[1], 128):
        there = (slice(None), slice(col, col + 128))
        here = (slice(None), slice(first + col, first + col + 128))
        grad = kept[there] + came[there]
        m = 0.9 * moment[here] + 0.1 * grad
        v = 0.95 * second[here] + 0.05 * grad * grad
        step = 0.3 * (m / (1.0 - 0.9**10))
        w = weights[here] - step / (jnp.sqrt(v / (1.0 - 0.95**10)) + 1e-08)
        new_moment[there] = m
        new_second[there] = v
        moved[there] = w
        total = total + w * w
    sums[...] = jnp.broadcast_to(jnp.sum(total, axis=1, keepdims=True), sums.shape)


def finish(name, after, cost, first, kept, came, weights, moment, second):
    shape = VMEM(kept.shape, F32)
    return call(
        functools.partial(finish_kernel, first),
        (kept, came, weights, moment, second),
        after,
        cost,
        out_shape=(shape, shape, shape, VMEM((ROWS, 128), F32)),
        out_specs=[in_vmem()] * 4,
        compiler_params=params(4),
        name=name,
    )


def join_kernel(a, b, c, d, ab, cd):
    width = a.shape[1]
    for left, right, out in ((a, b, ab), (c, d, cd)):
        out[:, :width] = left[...]
        out[:, width:] = right[...]


def join(after, moments, seconds):
    rows, width = moments[0].shape
    return call(
        join_kernel,
        (*moments, *seconds),
        after,
        1,
        out_shape=[jax.ShapeDtypeStruct((rows, 2 * width), F32)] * 2,
        out_specs=[in_vmem()] * 2,
        compiler_params=params(4),
        name="join",
    )


def rescale_kernel(width, a, b, *refs):
    *sums, out = refs
    total = sums[0][...]
    for other in sums[1:]:
        total = total + other[...]
    scale = lax.rsqrt(total / width + 1e-06)
    for k, moved in enumerate((a, b)):
        for col in range(0, moved.shape[1], 128):
            at = k * moved.shape[1] + col
            out[:, at : at + 128] = moved[:, col : col + 128] * scale


def rescale(moved, sums, width):
    rows, half = moved[0].shape
    return pl.pallas_call(
        functools.partial(rescale_kernel, width),
        out_shape=jax.ShapeDtypeStruct((rows, 2 * half), F32),
        in_specs=[in_vmem()] * (2 + len(sums)),
        out_specs=in_vmem(),
        compiler_params=params(4),
        name="rescale",
    )(*moved, *sums)


def on_device(out_grad, inputs, weights, moment, second):
    width = weights.shape[1] * lax.axis_size("tensor")
    out_grad, inputs = [pltpu.with_memory_space_constraint(z, pltpu.HBM) for z in (out_grad, inputs)]
    first = pieces_of(int(ORDER[0][-1]), "s", 1)
    turned, *halves, product = prep(out_grad, inputs, first)
    n = len(CHAINS)
    received, kept, came = {}, [None] * n, [None] * n
    late, done = {}, {}
    last = None
    for item in ORDER:
        what, which = item.split(":")
        which, _, shares = which.partition("/")
        shares = int(shares or 1)
        name = f"{what}_{which}"
        cost = COSTS.get(what + ":" + which, 1)
        chains = [int(i) for i in which]
        i = chains[0]
        order = CHAINS[i][3]
        if what[0] in "so":
            sent = int(what[1] == "1")
            pieces = [piece for j in chains for piece in pieces_of(j, what[0], sent)]
            if what[0] == "s":
                if shares > 1:
                    pieces = quarters(pieces)
                if last is None:
                    parts = [product]
                else:
                    parts = gemm(name, last, cost, turned, halves, pieces, shares)
                last = parts[0]
                over = [lax.ppermute(part, "dp", CORE_SWAP) for part in parts]
                for k, j in enumerate(chains):
                    received[j, sent] = over, k * (TILES // 2) * ROWS
            elif what[1] == "p":
                [last] = gemm(name, last, cost, turned, halves, pieces)
                kept[i] = last
            else:
                over, offset = received[i, sent]
                if len(over) > 1:
                    pieces = quarters(pieces)
                [last] = gemm(name, last, cost, turned, halves, pieces, 1, over, offset)
                if sent:
                    came[i] = lax.ppermute(last, "dp", SWAPS[order[0]])
                else:
                    kept[i] = last
        elif what == "x2":
            last = kept[i] = add(name, last, cost, kept[i], came[i])
            [came[i]], late[i] = received[i, 0]
        elif what == "f":
            first = i * kept[i].shape[1]
            done[i] = finish(name, last, cost, first, kept[i], came[i], weights, moment, second)
            last = done[i][3]
        else:
            step = int(what[1])
            split = 2 if step == 3 and order[2] == 3 else 1
            pairs = [(kept[j], came[j]) for j in chains]
            last, kept[i] = combine(name, last, cost, split, pairs, late.pop(i, 0))
            came[i] = lax.ppermute(last, "dp", SWAPS[order[step - 1]])
    moved, moments, seconds, sums = zip(done[0], done[1])
    sums = sums[0] + sums[1]
    new_moment, new_second = join(sums, moments, seconds)
    sums = [sums] + [lax.ppermute(sums, "tensor", swap) for swap in Z_SWAPS]
    return rescale(moved, sums, width), new_moment, new_second


def solution(mesh):
    spec = P("dp", "tensor")
    return jax.shard_map(
        on_device,
        mesh=mesh,
        in_specs=(P("dp", None), spec, spec, spec, spec),
        out_specs=(spec, spec, spec),
        check_vma=False,
    )
```

time: 170 us -> 84.1 us (0.49)
  waiting for transfers between devices: 118 us -> 29.1 us
  Pallas kernels: 0 us -> 28.1 us
  starting transfers between devices: 0.04 us -> 25.9 us
  matrix products: 24.3 us -> 0 us
  between operations: 14 us -> 0.87 us
  blocking collectives: 10.7 us -> 0 us
  other arithmetic: 3.39 us -> 0.01 us
    reduce_scatter x1 -> x0, waiting for transfers between devices: 118 us -> none  [on_device(): lax.psum_scatter(lax.dot_general(out_grad, inputs, (((0,), (0,)), ((), ()...]
    ppermute x0 -> x20, waiting for transfers between devices: none -> 29.1 us  [the longest x8 20.9 us: on_device(): came[i] = lax.ppermute(last, 'dp', SWAPS[order[step - 1]])]
    pallas_call x0 -> x27, Pallas kernels: none -> 28.1 us  [the longest x25 20.5 us: call(): pl.pallas_call(run, in_specs=specs, cost_estimate=cost, **more)]
    ppermute x0 -> x20, starting transfers between devices: none -> 25.9 us  [the longest x8 12.1 us: on_device(): came[i] = lax.ppermute(last, 'dp', SWAPS[order[step - 1]])]
    dot_general x1 -> x0, matrix products: 24.3 us -> none  [on_device(): lax.dot_general(out_grad, inputs, (((0,), (0,)), ((), ())), preferred_ele...]
    psum x1 -> x0, blocking collectives: 10.7 us -> none  [on_device(): totals = lax.psum(jnp.sum(moved * moved, axis=1), 'tensor')]
    reduce_sum x1 -> x0, other arithmetic: 2.47 us -> none  [on_device(): totals = lax.psum(jnp.sum(moved * moved, axis=1), 'tensor')]
  transfers between devices with their start and end apart: 1 -> 20, of which waited for: 1 -> 10; matrix products, arithmetic and copies ran while one was open for 0% -> 0% of each run, Pallas kernels for 0% -> 24%
where the time goes in v2:
time: 84.1 us; the launch traced here: 84 us
  waiting for transfers between devices  29.1 us (35%)
  Pallas kernels  28.1 us (33%)
  starting transfers between devices  25.9 us (31%)
  between operations  0.87 us (1%)
    ppermute x8, waiting for transfers between devices, on_device(): came[i] = lax.ppermute(last, 'dp', SWAPS[order[step - 1]])  20.9 us
    pallas_call x25, Pallas kernels, call(): pl.pallas_call(run, in_specs=specs, cost_estimate=cost, **more)  20.5 us
    ppermute x8, starting transfers between devices, on_device(): came[i] = lax.ppermute(last, 'dp', SWAPS[order[step - 1]])  12.1 us
    ppermute x4, starting transfers between devices, on_device(): came[i] = lax.ppermute(last, 'dp', SWAPS[order[0]])  6.95 us
    pallas_call x1, Pallas kernels, prep(): pl.pallas_call(functools.partial(prep_kernel, pieces), out_shape=(VMEM((2...  6.73 us
    ppermute x3, starting transfers between devices, on_device(): sums = [sums] + [lax.ppermute(sums, 'tensor', swap) for swap in Z_SWAPS]  4.93 us
    ppermute x3, waiting for transfers between devices, on_device(): sums = [sums] + [lax.ppermute(sums, 'tensor', swap) for swap in Z_SWAPS]  3.07 us
    ppermute x5, waiting for transfers between devices, on_device(): over = [lax.ppermute(part, 'dp', CORE_SWAP) for part in parts]  2.75 us
  transfers between devices with their start and end apart: 20, of which 10 were waited for; matrix products, arithmetic and copies ran while one was open for 0% of the time, Pallas kernels for 24%

profile of v2, /device:TPU:0, one launch (start us, length us, event | category | flops | bytes accessed | tf_op | source)
XLA Modules:
  0.0 84.0 jit_solution(7694907640598131247)
XLA Ops:
  0.6 6.7 %prep.1 = (bf16[32,64,2048]{2,1,0:T(8,128)(2,1)S(1)}, bf16[2048,1024]{1,0:T(8,128)(2,1)S(1)}, bf16[2048,1024]{1,0:T(8,128)(2,1)S(1)}, f32[512,768]{1,0:T(8,128)S(1)}) custom-call(bf16[2048,2048]{1,0:T(8,128)(2,1)} %out_grad.1, bf16[2048,2048]{1,0:T(8,128)(2,1)} %inputs.1), custom_call_target="tpu_custom_call" | custom-call | tf_op jit(solution)/shard_map/prep/pallas_call | solution.py:118
  7.5 1.8 %s1_1.1.refs_4_ = f32[512,768]{1,0:T(8,128)S(1)} custom-call(bf16[32,64,2048]{2,1,0:T(8,128)(2,1)S(1)} %get-tuple-element.33.refs_0_, bf16[2048,1024]{1,0:T(8,128)(2,1)S(1)} %get-tuple-element.34.refs_1_, bf16[2048,1024]{1,0:T(8,128)(2,1)S(1)} %get-tuple-element.35.refs_2_, f32[512,768]{1,0:T(8,128)S(1)} %get-tuple-element.36.refs_3_), custom_call_target="tpu_custom_call" | custom-call | flops 1 | bytes 1 | tf_op jit(solution)/shard_map/s1_1/pallas_call | solution.py:140
  10.9 1.8 %o1_0.1.refs_4_ = f32[512,768]{1,0:T(8,128)S(1)} custom-call(bf16[32,64,2048]{2,1,0:T(8,128)(2,1)S(1)} %get-tuple-element.33.refs_0_, bf16[2048,1024]{1,0:T(8,128)(2,1)S(1)} %get-tuple-element.34.refs_1_, bf16[2048,1024]{1,0:T(8,128)(2,1)S(1)} %get-tuple-element.35.refs_2_, f32[512,768]{1,0:T(8,128)S(1)} %collective-permute-done.1.refs_3_, ...), custom_call_target="tpu_custom_call" | custom-call | flops 1 | bytes 1 | tf_op jit(solution)/shard_map/o1_0/pallas_call | solution.py:140
  12.7 1.7 %collective-permute-start.2 = (f32[512,768]{1,0:T(8,128)S(1)}, f32[512,768]{1,0:T(8,128)S(1)}, u32[]{:S(2)}, u32[]{:S(2)}) collective-permute-start(f32[512,768]{1,0:T(8,128)S(1)} %o1_0.1.refs_4_), channel_id=1, source_target_pairs={{0,8},{4,36},{8,0},{12,44},{16,24},{20,52},{24,16},{28,60},{32,40}... | collective-permute-start | bytes 4718600 | tf_op jit(solution)/shard_map/ppermute | solution.py:353
  14.3 1.8 %o1_1.1.refs_3_ = f32[512,768]{1,0:T(8,128)S(1)} custom-call(bf16[32,64,2048]{2,1,0:T(8,128)(2,1)S(1)} %get-tuple-element.33.refs_0_, bf16[2048,1024]{1,0:T(8,128)(2,1)S(1)} %get-tuple-element.34.refs_1_, bf16[2048,1024]{1,0:T(8,128)(2,1)S(1)} %get-tuple-element.35.refs_2_, f32[512,768]{1,0:T(8,128)S(1)} %collective-permute-done.refs_3_, ...), custom_call_target="tpu_custom_call" | custom-call | flops 1 | bytes 1 | tf_op jit(solution)/shard_map/o1_1/pallas_call | solution.py:140
  16.1 2.2 %collective-permute-start.5 = (f32[512,768]{1,0:T(8,128)S(1)}, f32[512,768]{1,0:T(8,128)S(1)}, u32[]{:S(2)}, u32[]{:S(2)}) collective-permute-start(f32[512,768]{1,0:T(8,128)S(1)} %o1_1.1.refs_3_), channel_id=1, source_target_pairs={{0,24},{4,100},{8,16},{12,108},{16,8},{20,116},{24,0},{28,124},{32... | collective-permute-start | bytes 4718600 | tf_op jit(solution)/shard_map/ppermute | solution.py:353
  18.3 3.4 %s0_01.1.refs_3_ = f32[1024,768]{1,0:T(8,128)S(1)} custom-call(bf16[32,64,2048]{2,1,0:T(8,128)(2,1)S(1)} %get-tuple-element.33.refs_0_, bf16[2048,1024]{1,0:T(8,128)(2,1)S(1)} %get-tuple-element.34.refs_1_, bf16[2048,1024]{1,0:T(8,128)(2,1)S(1)} %get-tuple-element.35.refs_2_, f32[512,768]{1,0:T(8,128)S(1)} %o1_1.1.refs_3_), custom_call_target="tpu_custom_call" | custom-call | flops 1 | bytes 1 | tf_op jit(solution)/shard_map/s0_01/pallas_call | solution.py:140
  22.0 1.3 %s1_23.1.refs_3_ = f32[1024,256]{1,0:T(8,128)S(1)} custom-call(bf16[32,64,2048]{2,1,0:T(8,128)(2,1)S(1)} %get-tuple-element.33.refs_0_, bf16[2048,1024]{1,0:T(8,128)(2,1)S(1)} %get-tuple-element.34.refs_1_, bf16[2048,1024]{1,0:T(8,128)(2,1)S(1)} %get-tuple-element.35.refs_2_, f32[1024,768]{1,0:T(8,128)S(1)} %s0_01.1.refs_3_), custom_call_target="tpu_custom_call" | custom-call | flops 1 | bytes 1 | tf_op jit(solution)/shard_map/s1_23/pallas_call | solution.py:140
  23.8 1.8 %op_0.1.refs_3_.refs_0_ = f32[512,768]{1,0:T(8,128)S(1)} custom-call(bf16[32,64,2048]{2,1,0:T(8,128)(2,1)S(1)} %get-tuple-element.33.refs_0_, bf16[2048,1024]{1,0:T(8,128)(2,1)S(1)} %get-tuple-element.34.refs_1_, bf16[2048,1024]{1,0:T(8,128)(2,1)S(1)} %get-tuple-element.35.refs_2_, f32[1024,256]{1,0:T(8,128)S(1)} %s1_23.1.refs_3_), custom_call_target="tpu_custom_call" | custom-call | flops 1 | bytes 1 | tf_op jit(solution)/shard_map/op_0/pallas_call | solution.py:140
  25.6 1.8 %op_1.1.refs_4_.refs_0_ = f32[512,768]{1,0:T(8,128)S(1)} custom-call(bf16[32,64,2048]{2,1,0:T(8,128)(2,1)S(1)} %get-tuple-element.33.refs_0_, bf16[2048,1024]{1,0:T(8,128)(2,1)S(1)} %get-tuple-element.34.refs_1_, bf16[2048,1024]{1,0:T(8,128)(2,1)S(1)} %get-tuple-element.35.refs_2_, f32[512,768]{1,0:T(8,128)S(1)} %op_0.1.refs_3_.refs_0_), custom_call_target="tpu_custom_call" | custom-call | flops 1 | bytes 1 | tf_op jit(solution)/shard_map/op_1/pallas_call | solution.py:140
  27.4 1.7 %collective-permute-done.3.refs_3_ = f32[1024,256]{1,0:T(8,128)S(1)} collective-permute-done((f32[1024,256]{1,0:T(8,128)S(1)}, f32[1024,256]{1,0:T(8,128)S(1)}, u32[]{:S(2)}, u32[]{:S(2)}) %collective-permute-start.3) | collective-permute-done | bytes 1048608 | tf_op jit(solution)/shard_map/ppermute | solution.py:341
  31.5 2.2 %collective-permute-start.10 = (f32[512,256]{1,0:T(8,128)S(1)}, f32[512,256]{1,0:T(8,128)S(1)}, u32[]{:S(2)}, u32[]{:S(2)}) collective-permute-start(f32[512,256]{1,0:T(8,128)S(1)} %o1_3.1.refs_3_), channel_id=1, source_target_pairs={{0,24},{4,100},{8,16},{12,108},{16,8},{20,116},{24,0},{28,124},{32... | collective-permute-start | bytes 1572872 | tf_op jit(solution)/shard_map/ppermute | solution.py:353
  35.6 2.3 %collective-permute-done.5.refs_1_ = f32[512,768]{1,0:T(8,128)S(1)} collective-permute-done((f32[512,768]{1,0:T(8,128)S(1)}, f32[512,768]{1,0:T(8,128)S(1)}, u32[]{:S(2)}, u32[]{:S(2)}) %collective-permute-start.5) | collective-permute-done | bytes 1572896 | tf_op jit(solution)/shard_map/ppermute | solution.py:353
  38.2 2.2 %collective-permute-start.6 = (f32[256,768]{1,0:T(8,128)S(1)}, f32[256,768]{1,0:T(8,128)S(1)}, u32[]{:S(2)}, u32[]{:S(2)}) collective-permute-start(f32[256,768]{1,0:T(8,128)S(1)} %get-tuple-element.38.refs_2_), channel_id=1, source_target_pairs={{0,24},{4,100},{8,16},{12,108},{16,8},{20,116},{24,0},{28,124},{32... | collective-permute-start | bytes 2359304 | tf_op jit(solution)/shard_map/ppermute | solution.py:368
  43.5 1.4 %collective-permute-start.13 = (f32[256,256]{1,0:T(8,128)S(1)}, f32[256,256]{1,0:T(8,128)S(1)}, u32[]{:S(2)}, u32[]{:S(2)}) collective-permute-start(f32[256,256]{1,0:T(8,128)S(1)} %get-tuple-element.42.refs_4_), channel_id=1, source_target_pairs={{0,8},{4,36},{8,0},{12,44},{16,24},{20,52},{24,16},{28,60},{32,40}... | collective-permute-start | bytes 786440 | tf_op jit(solution)/shard_map/ppermute | solution.py:368
  44.9 9.8 %collective-permute-done.9.refs_3_ = f32[256,256]{1,0:T(8,128)S(1)} collective-permute-done((f32[256,256]{1,0:T(8,128)S(1)}, f32[256,256]{1,0:T(8,128)S(1)}, u32[]{:S(2)}, u32[]{:S(2)}) %collective-permute-start.9) | collective-permute-done | bytes 262176 | tf_op jit(solution)/shard_map/ppermute | solution.py:368
  54.8 1.7 %collective-permute-start.11 = (f32[128,1024]{1,0:T(8,128)S(1)}, f32[128,1024]{1,0:T(8,128)S(1)}, u32[]{:S(2)}, u32[]{:S(2)}) collective-permute-start(f32[128,1024]{1,0:T(8,128)S(1)} %get-tuple-element.44.refs_4_), channel_id=1, source_target_pairs={{0,32},{4,12},{8,40},{12,4},{16,48},{20,28},{24,56},{28,20},{32,0}... | collective-permute-start | bytes 1572872 | tf_op jit(solution)/shard_map/ppermute | solution.py:368
  56.6 2.3 %collective-permute-start.15 = (f32[128,1024]{1,0:T(8,128)S(1)}, f32[128,1024]{1,0:T(8,128)S(1)}, u32[]{:S(2)}, u32[]{:S(2)}) collective-permute-start(f32[128,1024]{1,0:T(8,128)S(1)} %get-tuple-element.47.refs_2_), channel_id=1, source_target_pairs={{0,96},{4,28},{8,104},{12,20},{16,112},{20,12},{24,120},{28,4},{32... | collective-permute-start | bytes 1572872 | tf_op jit(solution)/shard_map/ppermute | solution.py:368
  58.9 5.2 %collective-permute-done.11.refs_1_ = f32[128,1024]{1,0:T(8,128)S(1)} collective-permute-done((f32[128,1024]{1,0:T(8,128)S(1)}, f32[128,1024]{1,0:T(8,128)S(1)}, u32[]{:S(2)}, u32[]{:S(2)}) %collective-permute-start.11) | collective-permute-done | bytes 524320 | tf_op jit(solution)/shard_map/ppermute | solution.py:368
  64.1 3.1 %collective-permute-start.14 = (f32[64,1024]{1,0:T(8,128)S(1)}, f32[64,1024]{1,0:T(8,128)S(1)}, u32[]{:S(2)}, u32[]{:S(2)}) collective-permute-start(f32[64,1024]{1,0:T(8,128)S(1)} %get-tuple-element.49.refs_2_), channel_id=1, source_target_pairs={{0,96},{4,28},{8,104},{12,20},{16,112},{20,12},{24,120},{28,4},{32... | collective-permute-start | bytes 786440 | tf_op jit(solution)/shard_map/ppermute | solution.py:368
  67.5 4.3 %collective-permute-done.14.refs_1_ = f32[64,1024]{1,0:T(8,128)S(1)} collective-permute-done((f32[64,1024]{1,0:T(8,128)S(1)}, f32[64,1024]{1,0:T(8,128)S(1)}, u32[]{:S(2)}, u32[]{:S(2)}) %collective-permute-start.14) | collective-permute-done | bytes 262176 | tf_op jit(solution)/shard_map/ppermute | solution.py:368
  72.2 1.6 %collective-permute-done.16.refs_1_ = f32[64,1024]{1,0:T(8,128)S(1)} collective-permute-done((f32[64,1024]{1,0:T(8,128)S(1)}, f32[64,1024]{1,0:T(8,128)S(1)}, u32[]{:S(2)}, u32[]{:S(2)}) %collective-permute-start.16) | collective-permute-done | bytes 262176 | tf_op jit(solution)/shard_map/ppermute | solution.py:368
  74.1 3.9 %collective-permute-start.19 = (f32[64,128]{1,0:T(8,128)S(1)}, f32[64,128]{1,0:T(8,128)S(1)}, u32[]{:S(2)}, u32[]{:S(2)}) collective-permute-start(f32[64,128]{1,0:T(8,128)S(1)} %add.3.refs_0_.refs_4_), channel_id=1, source_target_pairs={{0,2},{1,3},{2,0},{3,1},{4,6},{5,7},{6,4},{7,5},{8,10},{9,11},{10,... | collective-permute-start | bytes 98312 | tf_op jit(solution)/shard_map/ppermute | solution.py:372
  80.2 2.9 %collective-permute-done.18.refs_2_ = f32[64,128]{1,0:T(8,128)S(1)} collective-permute-done((f32[64,128]{1,0:T(8,128)S(1)}, f32[64,128]{1,0:T(8,128)S(1)}, u32[]{:S(2)}, u32[]{:S(2)}) %collective-permute-start.18) | collective-permute-done | bytes 32800 | tf_op jit(solution)/shard_map/ppermute | solution.py:372
  (50 shorter events, 14.6 us)
Async XLA Ops:
  7.4 3.5 %collective-permute-start.1 = (f32[512,768]{1,0:T(8,128)S(1)}, f32[512,768]{1,0:T(8,128)S(1)}, u32[]{:S(2)}, u32[]{:S(2)}) collective-permute-start(f32[512,768]{1,0:T(8,128)S(1)} %get-tuple-element.36.refs_3_), channel_id=1, source_target_pairs={{0,4},{4,0},{8,12},{12,8},{16,20},{20,16},{24,28},{28,24},{32,36},... | collective-permute-start | bytes 4718600 | tf_op jit(solution)/shard_map/ppermute | solution.py:341
  9.3 5.1 %collective-permute-start = (f32[512,768]{1,0:T(8,128)S(1)}, f32[512,768]{1,0:T(8,128)S(1)}, u32[]{:S(2)}, u32[]{:S(2)}) collective-permute-start(f32[512,768]{1,0:T(8,128)S(1)} %s1_1.1.refs_4_), channel_id=1, source_target_pairs={{0,4},{4,0},{8,12},{12,8},{16,20},{20,16},{24,28},{28,24},{32,36},... | collective-permute-start | bytes 4718600 | tf_op jit(solution)/shard_map/ppermute | solution.py:341
  12.7 22.3 %collective-permute-start.2 = (f32[512,768]{1,0:T(8,128)S(1)}, f32[512,768]{1,0:T(8,128)S(1)}, u32[]{:S(2)}, u32[]{:S(2)}) collective-permute-start(f32[512,768]{1,0:T(8,128)S(1)} %o1_0.1.refs_4_), channel_id=1, source_target_pairs={{0,8},{4,36},{8,0},{12,44},{16,24},{20,52},{24,16},{28,60},{32,40}... | collective-permute-start | bytes 4718600 | tf_op jit(solution)/shard_map/ppermute | solution.py:353
  16.1 21.7 %collective-permute-start.5 = (f32[512,768]{1,0:T(8,128)S(1)}, f32[512,768]{1,0:T(8,128)S(1)}, u32[]{:S(2)}, u32[]{:S(2)}) collective-permute-start(f32[512,768]{1,0:T(8,128)S(1)} %o1_1.1.refs_3_), channel_id=1, source_target_pairs={{0,24},{4,100},{8,16},{12,108},{16,8},{20,116},{24,0},{28,124},{32... | collective-permute-start | bytes 4718600 | tf_op jit(solution)/shard_map/ppermute | solution.py:353
  21.7 16.3 %collective-permute-start.4 = (f32[1024,768]{1,0:T(8,128)S(1)}, f32[1024,768]{1,0:T(8,128)S(1)}, u32[]{:S(2)}, u32[]{:S(2)}) collective-permute-start(f32[1024,768]{1,0:T(8,128)S(1)} %s0_01.1.refs_3_), channel_id=1, source_target_pairs={{0,4},{4,0},{8,12},{12,8},{16,20},{20,16},{24,28},{28,24},{32,36},... | collective-permute-start | bytes 9437192 | tf_op jit(solution)/shard_map/ppermute | solution.py:341
  23.2 5.9 %collective-permute-start.3 = (f32[1024,256]{1,0:T(8,128)S(1)}, f32[1024,256]{1,0:T(8,128)S(1)}, u32[]{:S(2)}, u32[]{:S(2)}) collective-permute-start(f32[1024,256]{1,0:T(8,128)S(1)} %s1_23.1.refs_3_), channel_id=1, source_target_pairs={{0,4},{4,0},{8,12},{12,8},{16,20},{20,16},{24,28},{28,24},{32,36},... | collective-permute-start | bytes 3145736 | tf_op jit(solution)/shard_map/ppermute | solution.py:341
  29.8 12.2 %collective-permute-start.8 = (f32[512,256]{1,0:T(8,128)S(1)}, f32[512,256]{1,0:T(8,128)S(1)}, u32[]{:S(2)}, u32[]{:S(2)}) collective-permute-start(f32[512,256]{1,0:T(8,128)S(1)} %o1_2.1.refs_4_), channel_id=1, source_target_pairs={{0,8},{4,36},{8,0},{12,44},{16,24},{20,52},{24,16},{28,60},{32,40}... | collective-permute-start | bytes 1572872 | tf_op jit(solution)/shard_map/ppermute | solution.py:353
  31.5 11.9 %collective-permute-start.10 = (f32[512,256]{1,0:T(8,128)S(1)}, f32[512,256]{1,0:T(8,128)S(1)}, u32[]{:S(2)}, u32[]{:S(2)}) collective-permute-start(f32[512,256]{1,0:T(8,128)S(1)} %o1_3.1.refs_3_), channel_id=1, source_target_pairs={{0,24},{4,100},{8,16},{12,108},{16,8},{20,116},{24,0},{28,124},{32... | collective-permute-start | bytes 1572872 | tf_op jit(solution)/shard_map/ppermute | solution.py:353
  35.0 5.7 %collective-permute-start.7 = (f32[1024,256]{1,0:T(8,128)S(1)}, f32[1024,256]{1,0:T(8,128)S(1)}, u32[]{:S(2)}, u32[]{:S(2)}) collective-permute-start(f32[1024,256]{1,0:T(8,128)S(1)} %s0_23.1.refs_2_), channel_id=1, source_target_pairs={{0,4},{4,0},{8,12},{12,8},{16,20},{20,16},{24,28},{28,24},{32,36},... | collective-permute-start | bytes 3145736 | tf_op jit(solution)/shard_map/ppermute | solution.py:341
  38.2 16.5 %collective-permute-start.6 = (f32[256,768]{1,0:T(8,128)S(1)}, f32[256,768]{1,0:T(8,128)S(1)}, u32[]{:S(2)}, u32[]{:S(2)}) collective-permute-start(f32[256,768]{1,0:T(8,128)S(1)} %get-tuple-element.38.refs_2_), channel_id=1, source_target_pairs={{0,24},{4,100},{8,16},{12,108},{16,8},{20,116},{24,0},{28,124},{32... | collective-permute-start | bytes 2359304 | tf_op jit(solution)/shard_map/ppermute | solution.py:368
  40.5 16.0 %collective-permute-start.12 = (f32[256,768]{1,0:T(8,128)S(1)}, f32[256,768]{1,0:T(8,128)S(1)}, u32[]{:S(2)}, u32[]{:S(2)}) collective-permute-start(f32[256,768]{1,0:T(8,128)S(1)} %get-tuple-element.39.refs_4_), channel_id=1, source_target_pairs={{0,8},{4,36},{8,0},{12,44},{16,24},{20,52},{24,16},{28,60},{32,40}... | collective-permute-start | bytes 2359304 | tf_op jit(solution)/shard_map/ppermute | solution.py:368
  42.1 12.6 %collective-permute-start.9 = (f32[256,256]{1,0:T(8,128)S(1)}, f32[256,256]{1,0:T(8,128)S(1)}, u32[]{:S(2)}, u32[]{:S(2)}) collective-permute-start(f32[256,256]{1,0:T(8,128)S(1)} %get-tuple-element.41.refs_2_), channel_id=1, source_target_pairs={{0,24},{4,100},{8,16},{12,108},{16,8},{20,116},{24,0},{28,124},{32... | collective-permute-start | bytes 786440 | tf_op jit(solution)/shard_map/ppermute | solution.py:368
  43.5 13.0 %collective-permute-start.13 = (f32[256,256]{1,0:T(8,128)S(1)}, f32[256,256]{1,0:T(8,128)S(1)}, u32[]{:S(2)}, u32[]{:S(2)}) collective-permute-start(f32[256,256]{1,0:T(8,128)S(1)} %get-tuple-element.42.refs_4_), channel_id=1, source_target_pairs={{0,8},{4,36},{8,0},{12,44},{16,24},{20,52},{24,16},{28,60},{32,40}... | collective-permute-start | bytes 786440 | tf_op jit(solution)/shard_map/ppermute | solution.py:368
  54.8 9.3 %collective-permute-start.11 = (f32[128,1024]{1,0:T(8,128)S(1)}, f32[128,1024]{1,0:T(8,128)S(1)}, u32[]{:S(2)}, u32[]{:S(2)}) collective-permute-start(f32[128,1024]{1,0:T(8,128)S(1)} %get-tuple-element.44.refs_4_), channel_id=1, source_target_pairs={{0,32},{4,12},{8,40},{12,4},{16,48},{20,28},{24,56},{28,20},{32,0}... | collective-permute-start | bytes 1572872 | tf_op jit(solution)/shard_map/ppermute | solution.py:368
  56.6 15.2 %copy-start = (f32[64,2048]{1,0:T(8,128)S(1)}, f32[64,2048]{1,0:T(8,128)}, u32[]{:S(2)}) copy-start(f32[64,2048]{1,0:T(8,128)} %refs_2_.3) | copy-start | bytes 1572868
  56.6 15.2 %copy-start.1 = (f32[64,2048]{1,0:T(8,128)S(1)}, f32[64,2048]{1,0:T(8,128)}, u32[]{:S(2)}) copy-start(f32[64,2048]{1,0:T(8,128)} %refs_3_.3) | copy-start | bytes 1572868
  56.6 15.2 %copy-start.2 = (f32[64,2048]{1,0:T(8,128)S(1)}, f32[64,2048]{1,0:T(8,128)}, u32[]{:S(2)}) copy-start(f32[64,2048]{1,0:T(8,128)} %refs_4_.3) | copy-start | bytes 1572868
  56.6 10.6 %collective-permute-start.15 = (f32[128,1024]{1,0:T(8,128)S(1)}, f32[128,1024]{1,0:T(8,128)S(1)}, u32[]{:S(2)}, u32[]{:S(2)}) collective-permute-start(f32[128,1024]{1,0:T(8,128)S(1)} %get-tuple-element.47.refs_2_), channel_id=1, source_target_pairs={{0,96},{4,28},{8,104},{12,20},{16,112},{20,12},{24,120},{28,4},{32... | collective-permute-start | bytes 1572872 | tf_op jit(solution)/shard_map/ppermute | solution.py:368
  64.1 7.7 %collective-permute-start.14 = (f32[64,1024]{1,0:T(8,128)S(1)}, f32[64,1024]{1,0:T(8,128)S(1)}, u32[]{:S(2)}, u32[]{:S(2)}) collective-permute-start(f32[64,1024]{1,0:T(8,128)S(1)} %get-tuple-element.49.refs_2_), channel_id=1, source_target_pairs={{0,96},{4,28},{8,104},{12,20},{16,112},{20,12},{24,120},{28,4},{32... | collective-permute-start | bytes 786440 | tf_op jit(solution)/shard_map/ppermute | solution.py:368
  67.3 6.5 %collective-permute-start.16 = (f32[64,1024]{1,0:T(8,128)S(1)}, f32[64,1024]{1,0:T(8,128)S(1)}, u32[]{:S(2)}, u32[]{:S(2)}) collective-permute-start(f32[64,1024]{1,0:T(8,128)S(1)} %get-tuple-element.51.refs_5_), channel_id=1, source_target_pairs={{0,32},{4,12},{8,40},{12,4},{16,48},{20,28},{24,56},{28,20},{32,0}... | collective-permute-start | bytes 786440 | tf_op jit(solution)/shard_map/ppermute | solution.py:368
  74.1 6.2 %collective-permute-start.19 = (f32[64,128]{1,0:T(8,128)S(1)}, f32[64,128]{1,0:T(8,128)S(1)}, u32[]{:S(2)}, u32[]{:S(2)}) collective-permute-start(f32[64,128]{1,0:T(8,128)S(1)} %add.3.refs_0_.refs_4_), channel_id=1, source_target_pairs={{0,2},{1,3},{2,0},{3,1},{4,6},{5,7},{6,4},{7,5},{8,10},{9,11},{10,... | collective-permute-start | bytes 98312 | tf_op jit(solution)/shard_map/ppermute | solution.py:372
  78.0 5.1 %collective-permute-start.18 = (f32[64,128]{1,0:T(8,128)S(1)}, f32[64,128]{1,0:T(8,128)S(1)}, u32[]{:S(2)}, u32[]{:S(2)}) collective-permute-start(f32[64,128]{1,0:T(8,128)S(1)} %add.3.refs_0_.refs_4_), channel_id=1, source_target_pairs={{0,3},{1,2},{2,1},{3,0},{4,7},{5,6},{6,5},{7,4},{8,11},{9,10},{10,... | collective-permute-start | bytes 98312 | tf_op jit(solution)/shard_map/ppermute | solution.py:372
  78.7 4.4 %collective-permute-start.17 = (f32[64,128]{1,0:T(8,128)S(1)}, f32[64,128]{1,0:T(8,128)S(1)}, u32[]{:S(2)}, u32[]{:S(2)}) collective-permute-start(f32[64,128]{1,0:T(8,128)S(1)} %add.3.refs_0_.refs_4_), channel_id=1, source_target_pairs={{0,1},{1,0},{2,3},{3,2},{4,5},{5,4},{6,7},{7,6},{8,9},{9,8},{10,11... | collective-permute-start | bytes 98312 | tf_op jit(solution)/shard_map/ppermute | solution.py:372

commit v3 on v2

--- a/solution.py
+++ b/solution.py
@@ -16,13 +16,14 @@
 STRIPS = 8
 FORTH, BACK = (0, 1, 2, 3), (1, 0, 3, 2)
 CHAINS = ((0, 0, 768, FORTH), (1, 0, 768, BACK), (0, 768, 256, FORTH), (1, 768, 256, BACK))
+PARTS = [sum(chain[2] for chain in CHAINS if chain[0] == part) for part in (0, 1)]
 ORDER = (
-    "s1:0", "s1:1", "o1:0", "o1:1", "s0:01", "s1:23", "op:0", "op:1",
-    "o1:2", "o1:3", "s0:23", "x2:0", "x2:1", "c2:0", "c2:1", "o0:2",
-    "o0:3", "c2:2", "c2:3", "c3:02", "c3:13", "c4:0", "c4:1", "f:0",
-    "f:1",
+    "s1:0", "s1:1", "oq:0", "a1:0", "o1:1", "s0:01", "s1:23", "op:0",
+    "op:1", "o1:2", "o1:3", "s0:23", "x2:0", "x2:1", "c2:1", "c2:0",
+    "o0:2", "o0:3", "c2:3", "c2:2", "c3:13", "c3:02", "c4:1", "c4:0",
+    "f:1", "f:0",
 )
-COSTS = {"x2:1": 20000000000, "c2:1": 10000000000, "f:0": 1000000000}
+COSTS = {"x2:1": 20000000000, "c2:0": 10000000000, "f:1": 1000000000}
 
 RING_A = (1, 0, 3, 2)
 RING_B = (3, 2, 1, 0)
@@ -64,9 +65,10 @@
 
 def half_copies(inputs, half, which, arrived, first):
     rows, width = half.shape[0] // STRIPS, half.shape[1]
+    first_col = which * (inputs.shape[1] - width)
     return [
         pltpu.make_async_copy(
-            inputs.at[k * rows : (k + 1) * rows, which * width : (which + 1) * width],
+            inputs.at[k * rows : (k + 1) * rows, first_col : first_col + width],
             half.at[k * rows : (k + 1) * rows],
             arrived.at[first + k],
         )
@@ -113,11 +115,11 @@
 def prep(out_grad, inputs, pieces):
     tokens, rows = out_grad.shape
     strips = 8
-    half = VMEM((tokens, inputs.shape[1] // 2), BF16)
+    parts = [VMEM((tokens, cols), BF16) for cols in PARTS]
     product = sum(hi - lo for (lo, hi), *_ in pieces) * ROWS, pieces[0][3]
     return pl.pallas_call(
         functools.partial(prep_kernel, pieces),
-        out_shape=(VMEM((2 * TILES, ROWS, tokens), BF16), half, half, VMEM(product, F32)),
+        out_shape=(VMEM((2 * TILES, ROWS, tokens), BF16), *parts, VMEM(product, F32)),
         in_specs=[pl.BlockSpec(memory_space=pl.ANY)] * 2,
         out_specs=[in_vmem()] * 4,
         scratch_shapes=[
@@ -148,13 +150,16 @@
         left = turned[lo:hi].reshape(rows, turned.shape[2])
         out, at = outs[row // outs[0].shape[0]], row % outs[0].shape[0]
         for col in range(0, width, 256):
-            right = halves[half][:, first + col : first + col + 256]
+            end = min(col + 256, width)
+            right = halves[half][:, first + col : first + end]
             part = jnp.dot(left, right, preferred_element_type=F32)
             if received:
                 from_row = offset + row
                 ref, come = received[from_row // received[0].shape[0]], from_row % received[0].shape[0]
-                part = part + ref[come : come + rows, col : col + 256]
-            out[at : at + rows, col : col + 256] = part
+                part = part + ref[come : come + rows, col:end]
+            out[at : at + rows, col:end] = part
+        if width < out.shape[1]:
+            out[at : at + rows, width:] = jnp.zeros((rows, out.shape[1] - width), F32)
         row += rows
 
 
@@ -165,7 +170,7 @@
         (turned, *halves, *received),
         after,
         cost,
-        out_shape=[VMEM((rows // shares, pieces[0][3]), F32)] * shares,
+        out_shape=[VMEM((rows // shares, max(piece[3] for piece in pieces)), F32)] * shares,
         out_specs=[in_vmem()] * shares,
         compiler_params=params(4),
         name=name,
@@ -203,26 +208,30 @@
     )
 
 
-def combine_kernel(split, offset, *refs):
-    *pairs, up, down = refs
+def combine_kernel(split, offset, added, *refs):
+    *refs, up, down = refs
     col = 0
-    for kept, came in zip(pairs[::2], pairs[1::2]):
+    for is_sum in added:
+        kept = refs.pop(0)
+        came = None if is_sum else refs.pop(0)
         rows, width = kept.shape
         size = rows // (2 * split)
         for i in range(split):
             for half, out in ((0, down), (1, up)):
                 lo = (2 * i + half) * size
-                out[i * size : (i + 1) * size, col : col + width] = (
-                    kept[lo : lo + size] + came[offset + lo : offset + lo + size]
-                )
+                total = kept[lo : lo + size]
+                if came is not None:
+                    total = total + came[offset + lo : offset + lo + size, :width]
+                out[i * size : (i + 1) * size, col : col + width] = total
         col += width
 
 
 def combine(name, after, cost, split, pairs, offset=0):
     half = VMEM((pairs[0][0].shape[0] // 2, sum(kept.shape[1] for kept, _ in pairs)), F32)
+    added = [came is None for _, came in pairs]
     return call(
-        functools.partial(combine_kernel, split, offset),
-        [array for pair in pairs for array in pair],
+        functools.partial(combine_kernel, split, offset, added),
+        [array for pair in pairs for array in pair if array is not None],
         after,
         cost,
         out_shape=(half, half),
@@ -247,7 +256,8 @@
         new_second[there] = v
         moved[there] = w
         total = total + w * w
-    sums[...] = jnp.broadcast_to(jnp.sum(total, axis=1, keepdims=True), sums.shape)
+    total = jnp.broadcast_to(jnp.sum(total, axis=1, keepdims=True), total.shape)
+    sums[...] = total.T[: sums.shape[0]]
 
 
 def finish(name, after, cost, first, kept, came, weights, moment, second):
@@ -257,7 +267,7 @@
         (kept, came, weights, moment, second),
         after,
         cost,
-        out_shape=(shape, shape, shape, VMEM((ROWS, 128), F32)),
+        out_shape=(shape, shape, shape, VMEM((8, ROWS), F32)),
         out_specs=[in_vmem()] * 4,
         compiler_params=params(4),
         name=name,
@@ -272,13 +282,13 @@
 
 
 def join(after, moments, seconds):
-    rows, width = moments[0].shape
+    shape = jax.ShapeDtypeStruct((ROWS, sum(PARTS)), F32)
     return call(
         join_kernel,
         (*moments, *seconds),
         after,
         1,
-        out_shape=[jax.ShapeDtypeStruct((rows, 2 * width), F32)] * 2,
+        out_shape=[shape] * 2,
         out_specs=[in_vmem()] * 2,
         compiler_params=params(4),
         name="join",
@@ -290,18 +300,19 @@
     total = sums[0][...]
     for other in sums[1:]:
         total = total + other[...]
-    scale = lax.rsqrt(total / width + 1e-06)
-    for k, moved in enumerate((a, b)):
+    scale = lax.rsqrt(total[:1] / width + 1e-06)
+    scale = jnp.broadcast_to(scale, (128, ROWS)).T
+    at = 0
+    for moved in (a, b):
         for col in range(0, moved.shape[1], 128):
-            at = k * moved.shape[1] + col
-            out[:, at : at + 128] = moved[:, col : col + 128] * scale
+            out[:, at + col : at + col + 128] = moved[:, col : col + 128] * scale
+        at += moved.shape[1]
 
 
 def rescale(moved, sums, width):
-    rows, half = moved[0].shape
     return pl.pallas_call(
         functools.partial(rescale_kernel, width),
-        out_shape=jax.ShapeDtypeStruct((rows, 2 * half), F32),
+        out_shape=jax.ShapeDtypeStruct((ROWS, sum(PARTS)), F32),
         in_specs=[in_vmem()] * (2 + len(sums)),
         out_specs=in_vmem(),
         compiler_params=params(4),
@@ -316,7 +327,7 @@
     turned, *halves, product = prep(out_grad, inputs, first)
     n = len(CHAINS)
     received, kept, came = {}, [None] * n, [None] * n
-    late, done = {}, {}
+    late, own, done = {}, {}, {}
     last = None
     for item in ORDER:
         what, which = item.split(":")
@@ -344,6 +355,10 @@
             elif what[1] == "p":
                 [last] = gemm(name, last, cost, turned, halves, pieces)
                 kept[i] = last
+            elif what[1] == "q":
+                pieces = pieces_of(i, "o", 1)
+                [last] = gemm(name, last, cost, turned, halves, pieces)
+                own[i] = last
             else:
                 over, offset = received[i, sent]
                 if len(over) > 1:
@@ -353,11 +368,16 @@
                     came[i] = lax.ppermute(last, "dp", SWAPS[order[0]])
                 else:
                     kept[i] = last
-        elif what == "x2":
+        elif what == "a1":
+            last = add(name, last, cost, own[i], *received[i, 1][0])
+            came[i] = lax.ppermute(last, "dp", SWAPS[order[0]])
+        elif what[0] == "x":
             last = kept[i] = add(name, last, cost, kept[i], came[i])
-            [came[i]], late[i] = received[i, 0]
+            came[i] = None
+            if what == "x2":
+                [came[i]], late[i] = received[i, 0]
         elif what == "f":
-            first = i * kept[i].shape[1]
+            first = i * PARTS[0]
             done[i] = finish(name, last, cost, first, kept[i], came[i], weights, moment, second)
             last = done[i][3]
         else:

time: 84.1 us -> 82.7 us (0.983)
  waiting for transfers between devices: 29.1 us -> 28 us
    ppermute x8, starting transfers between devices: 12.1 us -> 11 us  [on_device(): came[i] = lax.ppermute(last, 'dp', SWAPS[order[step - 1]])]
    ppermute x5, waiting for transfers between devices: 2.75 us -> 1.72 us  [on_device(): over = [lax.ppermute(part, 'dp', CORE_SWAP) for part in parts]]
    pallas_call x25 -> x26, Pallas kernels: 20.5 us -> 20.8 us  [call(): pl.pallas_call(run, in_specs=specs, cost_estimate=cost, **more)]
  transfers between devices with their start and end apart: 20 -> 20, of which waited for: 10 -> 9; matrix products, arithmetic and copies ran while one was open for 0% -> 0% of each run, Pallas kernels for 24% -> 25%
where the time goes in v3:
time: 82.7 us; the launch traced here: 82.6 us
  Pallas kernels  28.4 us (34%)
  waiting for transfers between devices  28 us (34%)
  starting transfers between devices  25.2 us (30%)
  between operations  0.88 us (1%)
    pallas_call x26, Pallas kernels, call(): pl.pallas_call(run, in_specs=specs, cost_estimate=cost, **more)  20.8 us
    ppermute x8, waiting for transfers between devices, on_device(): came[i] = lax.ppermute(last, 'dp', SWAPS[order[step - 1]])  20.6 us
    ppermute x8, starting transfers between devices, on_device(): came[i] = lax.ppermute(last, 'dp', SWAPS[order[step - 1]])  11 us
    ppermute x4, starting transfers between devices, on_device(): came[i] = lax.ppermute(last, 'dp', SWAPS[order[0]])  7.7 us
    pallas_call x1, Pallas kernels, prep(): pl.pallas_call(functools.partial(prep_kernel, pieces), out_shape=(VMEM((2...  6.73 us
    ppermute x3, starting transfers between devices, on_device(): sums = [sums] + [lax.ppermute(sums, 'tensor', swap) for swap in Z_SWAPS]  4.9 us
    ppermute x4, waiting for transfers between devices, on_device(): came[i] = lax.ppermute(last, 'dp', SWAPS[order[0]])  2.89 us
    ppermute x3, waiting for transfers between devices, on_device(): sums = [sums] + [lax.ppermute(sums, 'tensor', swap) for swap in Z_SWAPS]  2.77 us
  transfers between devices with their start and end apart: 20, of which 9 were waited for; matrix products, arithmetic and copies ran while one was open for 0% of the time, Pallas kernels for 25%

profile of v3, /device:TPU:0, one launch (start us, length us, event | category | flops | bytes accessed | tf_op | source)
XLA Modules:
  0.0 82.6 jit_solution(8975894748551286926)
XLA Ops:
  0.6 6.7 %prep.1 = (bf16[32,64,2048]{2,1,0:T(8,128)(2,1)S(1)}, bf16[2048,1024]{1,0:T(8,128)(2,1)S(1)}, bf16[2048,1024]{1,0:T(8,128)(2,1)S(1)}, f32[512,768]{1,0:T(8,128)S(1)}) custom-call(bf16[2048,2048]{1,0:T(8,128)(2,1)} %out_grad.1, bf16[2048,2048]{1,0:T(8,128)(2,1)} %inputs.1), custom_call_target="tpu_custom_call" | custom-call | tf_op jit(solution)/shard_map/prep/pallas_call | solution.py:120
  7.5 1.8 %s1_1.1.refs_3_ = f32[512,768]{1,0:T(8,128)S(1)} custom-call(bf16[32,64,2048]{2,1,0:T(8,128)(2,1)S(1)} %get-tuple-element.33.refs_0_, bf16[2048,1024]{1,0:T(8,128)(2,1)S(1)} %get-tuple-element.34.refs_1_, bf16[2048,1024]{1,0:T(8,128)(2,1)S(1)} %get-tuple-element.35.refs_2_, f32[512,768]{1,0:T(8,128)S(1)} %get-tuple-element.36.refs_3_), custom_call_target="tpu_custom_call" | custom-call | flops 1 | bytes 1 | tf_op jit(solution)/shard_map/s1_1/pallas_call | solution.py:142
  9.8 1.8 %oq_0.1.refs_0_.refs_2_ = f32[512,768]{1,0:T(8,128)S(1)} custom-call(bf16[32,64,2048]{2,1,0:T(8,128)(2,1)S(1)} %get-tuple-element.33.refs_0_, bf16[2048,1024]{1,0:T(8,128)(2,1)S(1)} %get-tuple-element.34.refs_1_, bf16[2048,1024]{1,0:T(8,128)(2,1)S(1)} %get-tuple-element.35.refs_2_, f32[512,768]{1,0:T(8,128)S(1)} %s1_1.1.refs_3_), custom_call_target="tpu_custom_call" | custom-call | flops 1 | bytes 1 | tf_op jit(solution)/shard_map/oq_0/pallas_call | solution.py:142
  11.8 1.7 %collective-permute-start.2 = (f32[512,768]{1,0:T(8,128)S(1)}, f32[512,768]{1,0:T(8,128)S(1)}, u32[]{:S(2)}, u32[]{:S(2)}) collective-permute-start(f32[512,768]{1,0:T(8,128)S(1)} %a1_0.1.refs_4_), channel_id=1, source_target_pairs={{0,8},{4,36},{8,0},{12,44},{16,24},{20,52},{24,16},{28,60},{32,40}... | collective-permute-start | bytes 4718600 | tf_op jit(solution)/shard_map/ppermute | solution.py:373
  13.5 1.8 %o1_1.1.refs_3_ = f32[512,768]{1,0:T(8,128)S(1)} custom-call(bf16[32,64,2048]{2,1,0:T(8,128)(2,1)S(1)} %get-tuple-element.33.refs_0_, bf16[2048,1024]{1,0:T(8,128)(2,1)S(1)} %get-tuple-element.34.refs_1_, bf16[2048,1024]{1,0:T(8,128)(2,1)S(1)} %get-tuple-element.35.refs_2_, f32[512,768]{1,0:T(8,128)S(1)} %collective-permute-done.refs_3_, ...), custom_call_target="tpu_custom_call" | custom-call | flops 1 | bytes 1 | tf_op jit(solution)/shard_map/o1_1/pallas_call | solution.py:142
  15.3 2.6 %collective-permute-start.5 = (f32[512,768]{1,0:T(8,128)S(1)}, f32[512,768]{1,0:T(8,128)S(1)}, u32[]{:S(2)}, u32[]{:S(2)}) collective-permute-start(f32[512,768]{1,0:T(8,128)S(1)} %o1_1.1.refs_3_), channel_id=1, source_target_pairs={{0,24},{4,100},{8,16},{12,108},{16,8},{20,116},{24,0},{28,124},{32... | collective-permute-start | bytes 4718600 | tf_op jit(solution)/shard_map/ppermute | solution.py:368
  17.8 3.4 %s0_01.1.refs_3_ = f32[1024,768]{1,0:T(8,128)S(1)} custom-call(bf16[32,64,2048]{2,1,0:T(8,128)(2,1)S(1)} %get-tuple-element.33.refs_0_, bf16[2048,1024]{1,0:T(8,128)(2,1)S(1)} %get-tuple-element.34.refs_1_, bf16[2048,1024]{1,0:T(8,128)(2,1)S(1)} %get-tuple-element.35.refs_2_, f32[512,768]{1,0:T(8,128)S(1)} %o1_1.1.refs_3_), custom_call_target="tpu_custom_call" | custom-call | flops 1 | bytes 1 | tf_op jit(solution)/shard_map/s0_01/pallas_call | solution.py:142
  23.3 1.8 %op_0.1.refs_3_.refs_0_ = f32[512,768]{1,0:T(8,128)S(1)} custom-call(bf16[32,64,2048]{2,1,0:T(8,128)(2,1)S(1)} %get-tuple-element.33.refs_0_, bf16[2048,1024]{1,0:T(8,128)(2,1)S(1)} %get-tuple-element.34.refs_1_, bf16[2048,1024]{1,0:T(8,128)(2,1)S(1)} %get-tuple-element.35.refs_2_, f32[1024,256]{1,0:T(8,128)S(1)} %s1_23.1.refs_3_), custom_call_target="tpu_custom_call" | custom-call | flops 1 | bytes 1 | tf_op jit(solution)/shard_map/op_0/pallas_call | solution.py:142
  25.1 1.8 %op_1.1.refs_4_.refs_0_ = f32[512,768]{1,0:T(8,128)S(1)} custom-call(bf16[32,64,2048]{2,1,0:T(8,128)(2,1)S(1)} %get-tuple-element.33.refs_0_, bf16[2048,1024]{1,0:T(8,128)(2,1)S(1)} %get-tuple-element.34.refs_1_, bf16[2048,1024]{1,0:T(8,128)(2,1)S(1)} %get-tuple-element.35.refs_2_, f32[512,768]{1,0:T(8,128)S(1)} %op_0.1.refs_3_.refs_0_), custom_call_target="tpu_custom_call" | custom-call | flops 1 | bytes 1 | tf_op jit(solution)/shard_map/op_1/pallas_call | solution.py:142
  26.9 1.7 %collective-permute-done.3.refs_3_ = f32[1024,256]{1,0:T(8,128)S(1)} collective-permute-done((f32[1024,256]{1,0:T(8,128)S(1)}, f32[1024,256]{1,0:T(8,128)S(1)}, u32[]{:S(2)}, u32[]{:S(2)}) %collective-permute-start.3) | collective-permute-done | bytes 1048608 | tf_op jit(solution)/shard_map/ppermute | solution.py:352
  29.4 1.3 %collective-permute-start.8 = (f32[512,256]{1,0:T(8,128)S(1)}, f32[512,256]{1,0:T(8,128)S(1)}, u32[]{:S(2)}, u32[]{:S(2)}) collective-permute-start(f32[512,256]{1,0:T(8,128)S(1)} %o1_2.1.refs_4_), channel_id=1, source_target_pairs={{0,8},{4,36},{8,0},{12,44},{16,24},{20,52},{24,16},{28,60},{32,40}... | collective-permute-start | bytes 1572872 | tf_op jit(solution)/shard_map/ppermute | solution.py:368
  31.4 2.2 %collective-permute-start.9 = (f32[512,256]{1,0:T(8,128)S(1)}, f32[512,256]{1,0:T(8,128)S(1)}, u32[]{:S(2)}, u32[]{:S(2)}) collective-permute-start(f32[512,256]{1,0:T(8,128)S(1)} %o1_3.1.refs_3_), channel_id=1, source_target_pairs={{0,24},{4,100},{8,16},{12,108},{16,8},{20,116},{24,0},{28,124},{32... | collective-permute-start | bytes 1572872 | tf_op jit(solution)/shard_map/ppermute | solution.py:368
  35.1 1.9 %collective-permute-done.5.refs_1_ = f32[512,768]{1,0:T(8,128)S(1)} collective-permute-done((f32[512,768]{1,0:T(8,128)S(1)}, f32[512,768]{1,0:T(8,128)S(1)}, u32[]{:S(2)}, u32[]{:S(2)}) %collective-permute-start.5) | collective-permute-done | bytes 1572896 | tf_op jit(solution)/shard_map/ppermute | solution.py:368
  37.6 2.6 %collective-permute-start.6 = (f32[256,768]{1,0:T(8,128)S(1)}, f32[256,768]{1,0:T(8,128)S(1)}, u32[]{:S(2)}, u32[]{:S(2)}) collective-permute-start(f32[256,768]{1,0:T(8,128)S(1)} %get-tuple-element.39.refs_4_), channel_id=1, source_target_pairs={{0,24},{4,100},{8,16},{12,108},{16,8},{20,116},{24,0},{28,124},{32... | collective-permute-start | bytes 2359304 | tf_op jit(solution)/shard_map/ppermute | solution.py:388
  43.2 2.2 %collective-permute-start.10 = (f32[256,256]{1,0:T(8,128)S(1)}, f32[256,256]{1,0:T(8,128)S(1)}, u32[]{:S(2)}, u32[]{:S(2)}) collective-permute-start(f32[256,256]{1,0:T(8,128)S(1)} %get-tuple-element.42.refs_4_), channel_id=1, source_target_pairs={{0,24},{4,100},{8,16},{12,108},{16,8},{20,116},{24,0},{28,124},{32... | collective-permute-start | bytes 786440 | tf_op jit(solution)/shard_map/ppermute | solution.py:388
  45.4 6.8 %collective-permute-done.12.refs_3_ = f32[256,256]{1,0:T(8,128)S(1)} collective-permute-done((f32[256,256]{1,0:T(8,128)S(1)}, f32[256,256]{1,0:T(8,128)S(1)}, u32[]{:S(2)}, u32[]{:S(2)}) %collective-permute-start.12) | collective-permute-done | bytes 262176 | tf_op jit(solution)/shard_map/ppermute | solution.py:388
  52.3 3.1 %collective-permute-start.14 = (f32[128,1024]{1,0:T(8,128)S(1)}, f32[128,1024]{1,0:T(8,128)S(1)}, u32[]{:S(2)}, u32[]{:S(2)}) collective-permute-start(f32[128,1024]{1,0:T(8,128)S(1)} %get-tuple-element.45.refs_4_), channel_id=1, source_target_pairs={{0,96},{4,28},{8,104},{12,20},{16,112},{20,12},{24,120},{28,4},{32... | collective-permute-start | bytes 1572872 | tf_op jit(solution)/shard_map/ppermute | solution.py:388
  56.2 6.5 %collective-permute-done.14.refs_1_ = f32[128,1024]{1,0:T(8,128)S(1)} collective-permute-done((f32[128,1024]{1,0:T(8,128)S(1)}, f32[128,1024]{1,0:T(8,128)S(1)}, u32[]{:S(2)}, u32[]{:S(2)}) %collective-permute-start.14) | collective-permute-done | bytes 524320 | tf_op jit(solution)/shard_map/ppermute | solution.py:388
  63.3 1.5 %collective-permute-done.13.refs_1_ = f32[128,1024]{1,0:T(8,128)S(1)} collective-permute-done((f32[128,1024]{1,0:T(8,128)S(1)}, f32[128,1024]{1,0:T(8,128)S(1)}, u32[]{:S(2)}, u32[]{:S(2)}) %collective-permute-start.13) | collective-permute-done | bytes 524320 | tf_op jit(solution)/shard_map/ppermute | solution.py:388
  64.9 1.5 %collective-permute-start.15 = (f32[64,1024]{1,0:T(8,128)S(1)}, f32[64,1024]{1,0:T(8,128)S(1)}, u32[]{:S(2)}, u32[]{:S(2)}) collective-permute-start(f32[64,1024]{1,0:T(8,128)S(1)} %get-tuple-element.51.refs_5_), channel_id=1, source_target_pairs={{0,96},{4,28},{8,104},{12,20},{16,112},{20,12},{24,120},{28,4},{32... | collective-permute-start | bytes 786440 | tf_op jit(solution)/shard_map/ppermute | solution.py:388
  66.4 2.9 %collective-permute-done.16.refs_1_ = f32[64,1024]{1,0:T(8,128)S(1)} collective-permute-done((f32[64,1024]{1,0:T(8,128)S(1)}, f32[64,1024]{1,0:T(8,128)S(1)}, u32[]{:S(2)}, u32[]{:S(2)}) %collective-permute-start.16) | collective-permute-done | bytes 262176 | tf_op jit(solution)/shard_map/ppermute | solution.py:388
  69.7 2.8 %collective-permute-done.15.refs_1_ = f32[64,1024]{1,0:T(8,128)S(1)} collective-permute-done((f32[64,1024]{1,0:T(8,128)S(1)}, f32[64,1024]{1,0:T(8,128)S(1)}, u32[]{:S(2)}, u32[]{:S(2)}) %collective-permute-start.15) | collective-permute-done | bytes 262176 | tf_op jit(solution)/shard_map/ppermute | solution.py:388
  73.0 3.9 %collective-permute-start.19 = (f32[8,64]{1,0:T(8,128)S(1)}, f32[8,64]{1,0:T(8,128)S(1)}, u32[]{:S(2)}, u32[]{:S(2)}) collective-permute-start(f32[8,64]{1,0:T(8,128)S(1)} %add.3.refs_0_.refs_4_), channel_id=1, source_target_pairs={{0,2},{1,3},{2,0},{3,1},{4,6},{5,7},{6,4},{7,5},{8,10},{9,11},{10,... | collective-permute-start | bytes 6152 | tf_op jit(solution)/shard_map/ppermute | solution.py:392
  78.9 2.8 %collective-permute-done.18.refs_2_ = f32[8,64]{1,0:T(8,128)S(1)} collective-permute-done((f32[8,64]{1,0:T(8,128)S(1)}, f32[8,64]{1,0:T(8,128)S(1)}, u32[]{:S(2)}, u32[]{:S(2)}) %collective-permute-start.18) | collective-permute-done | bytes 2080 | tf_op jit(solution)/shard_map/ppermute | solution.py:392
  (51 shorter events, 14.7 us)
Async XLA Ops:
  7.4 4.3 %collective-permute-start.1 = (f32[512,768]{1,0:T(8,128)S(1)}, f32[512,768]{1,0:T(8,128)S(1)}, u32[]{:S(2)}, u32[]{:S(2)}) collective-permute-start(f32[512,768]{1,0:T(8,128)S(1)} %get-tuple-element.36.refs_3_), channel_id=1, source_target_pairs={{0,4},{4,0},{8,12},{12,8},{16,20},{20,16},{24,28},{28,24},{32,36},... | collective-permute-start | bytes 4718600 | tf_op jit(solution)/shard_map/ppermute | solution.py:352
  9.3 4.2 %collective-permute-start = (f32[512,768]{1,0:T(8,128)S(1)}, f32[512,768]{1,0:T(8,128)S(1)}, u32[]{:S(2)}, u32[]{:S(2)}) collective-permute-start(f32[512,768]{1,0:T(8,128)S(1)} %s1_1.1.refs_3_), channel_id=1, source_target_pairs={{0,4},{4,0},{8,12},{12,8},{16,20},{20,16},{24,28},{28,24},{32,36},... | collective-permute-start | bytes 4718600 | tf_op jit(solution)/shard_map/ppermute | solution.py:352
  11.8 23.0 %collective-permute-start.2 = (f32[512,768]{1,0:T(8,128)S(1)}, f32[512,768]{1,0:T(8,128)S(1)}, u32[]{:S(2)}, u32[]{:S(2)}) collective-permute-start(f32[512,768]{1,0:T(8,128)S(1)} %a1_0.1.refs_4_), channel_id=1, source_target_pairs={{0,8},{4,36},{8,0},{12,44},{16,24},{20,52},{24,16},{28,60},{32,40}... | collective-permute-start | bytes 4718600 | tf_op jit(solution)/shard_map/ppermute | solution.py:373
  15.3 21.7 %collective-permute-start.5 = (f32[512,768]{1,0:T(8,128)S(1)}, f32[512,768]{1,0:T(8,128)S(1)}, u32[]{:S(2)}, u32[]{:S(2)}) collective-permute-start(f32[512,768]{1,0:T(8,128)S(1)} %o1_1.1.refs_3_), channel_id=1, source_target_pairs={{0,24},{4,100},{8,16},{12,108},{16,8},{20,116},{24,0},{28,124},{32... | collective-permute-start | bytes 4718600 | tf_op jit(solution)/shard_map/ppermute | solution.py:368
  21.2 15.9 %collective-permute-start.4 = (f32[1024,768]{1,0:T(8,128)S(1)}, f32[1024,768]{1,0:T(8,128)S(1)}, u32[]{:S(2)}, u32[]{:S(2)}) collective-permute-start(f32[1024,768]{1,0:T(8,128)S(1)} %s0_01.1.refs_3_), channel_id=1, source_target_pairs={{0,4},{4,0},{8,12},{12,8},{16,20},{20,16},{24,28},{28,24},{32,36},... | collective-permute-start | bytes 9437192 | tf_op jit(solution)/shard_map/ppermute | solution.py:352
  22.9 5.8 %collective-permute-start.3 = (f32[1024,256]{1,0:T(8,128)S(1)}, f32[1024,256]{1,0:T(8,128)S(1)}, u32[]{:S(2)}, u32[]{:S(2)}) collective-permute-start(f32[1024,256]{1,0:T(8,128)S(1)} %s1_23.1.refs_3_), channel_id=1, source_target_pairs={{0,4},{4,0},{8,12},{12,8},{16,20},{20,16},{24,28},{28,24},{32,36},... | collective-permute-start | bytes 3145736 | tf_op jit(solution)/shard_map/ppermute | solution.py:352
  29.4 13.8 %collective-permute-start.8 = (f32[512,256]{1,0:T(8,128)S(1)}, f32[512,256]{1,0:T(8,128)S(1)}, u32[]{:S(2)}, u32[]{:S(2)}) collective-permute-start(f32[512,256]{1,0:T(8,128)S(1)} %o1_2.1.refs_4_), channel_id=1, source_target_pairs={{0,8},{4,36},{8,0},{12,44},{16,24},{20,52},{24,16},{28,60},{32,40}... | collective-permute-start | bytes 1572872 | tf_op jit(solution)/shard_map/ppermute | solution.py:368
  31.4 11.2 %collective-permute-start.9 = (f32[512,256]{1,0:T(8,128)S(1)}, f32[512,256]{1,0:T(8,128)S(1)}, u32[]{:S(2)}, u32[]{:S(2)}) collective-permute-start(f32[512,256]{1,0:T(8,128)S(1)} %o1_3.1.refs_3_), channel_id=1, source_target_pairs={{0,24},{4,100},{8,16},{12,108},{16,8},{20,116},{24,0},{28,124},{32... | collective-permute-start | bytes 1572872 | tf_op jit(solution)/shard_map/ppermute | solution.py:368
  34.8 5.3 %collective-permute-start.7 = (f32[1024,256]{1,0:T(8,128)S(1)}, f32[1024,256]{1,0:T(8,128)S(1)}, u32[]{:S(2)}, u32[]{:S(2)}) collective-permute-start(f32[1024,256]{1,0:T(8,128)S(1)} %s0_23.1.refs_2_), channel_id=1, source_target_pairs={{0,4},{4,0},{8,12},{12,8},{16,20},{20,16},{24,28},{28,24},{32,36},... | collective-permute-start | bytes 3145736 | tf_op jit(solution)/shard_map/ppermute | solution.py:352
  37.3 14.9 %collective-permute-start.11 = (f32[256,768]{1,0:T(8,128)S(1)}, f32[256,768]{1,0:T(8,128)S(1)}, u32[]{:S(2)}, u32[]{:S(2)}) collective-permute-start(f32[256,768]{1,0:T(8,128)S(1)} %get-tuple-element.37.refs_2_), channel_id=1, source_target_pairs={{0,8},{4,36},{8,0},{12,44},{16,24},{20,52},{24,16},{28,60},{32,40}... | collective-permute-start | bytes 2359304 | tf_op jit(solution)/shard_map/ppermute | solution.py:388
  37.6 17.8 %collective-permute-start.6 = (f32[256,768]{1,0:T(8,128)S(1)}, f32[256,768]{1,0:T(8,128)S(1)}, u32[]{:S(2)}, u32[]{:S(2)}) collective-permute-start(f32[256,768]{1,0:T(8,128)S(1)} %get-tuple-element.39.refs_4_), channel_id=1, source_target_pairs={{0,24},{4,100},{8,16},{12,108},{16,8},{20,116},{24,0},{28,124},{32... | collective-permute-start | bytes 2359304 | tf_op jit(solution)/shard_map/ppermute | solution.py:388
  42.6 9.5 %collective-permute-start.12 = (f32[256,256]{1,0:T(8,128)S(1)}, f32[256,256]{1,0:T(8,128)S(1)}, u32[]{:S(2)}, u32[]{:S(2)}) collective-permute-start(f32[256,256]{1,0:T(8,128)S(1)} %get-tuple-element.40.refs_2_), channel_id=1, source_target_pairs={{0,8},{4,36},{8,0},{12,44},{16,24},{20,52},{24,16},{28,60},{32,40}... | collective-permute-start | bytes 786440 | tf_op jit(solution)/shard_map/ppermute | solution.py:388
  43.2 12.2 %collective-permute-start.10 = (f32[256,256]{1,0:T(8,128)S(1)}, f32[256,256]{1,0:T(8,128)S(1)}, u32[]{:S(2)}, u32[]{:S(2)}) collective-permute-start(f32[256,256]{1,0:T(8,128)S(1)} %get-tuple-element.42.refs_4_), channel_id=1, source_target_pairs={{0,24},{4,100},{8,16},{12,108},{16,8},{20,116},{24,0},{28,124},{32... | collective-permute-start | bytes 786440 | tf_op jit(solution)/shard_map/ppermute | solution.py:388
  52.3 10.5 %collective-permute-start.14 = (f32[128,1024]{1,0:T(8,128)S(1)}, f32[128,1024]{1,0:T(8,128)S(1)}, u32[]{:S(2)}, u32[]{:S(2)}) collective-permute-start(f32[128,1024]{1,0:T(8,128)S(1)} %get-tuple-element.45.refs_4_), channel_id=1, source_target_pairs={{0,96},{4,28},{8,104},{12,20},{16,112},{20,12},{24,120},{28,4},{32... | collective-permute-start | bytes 1572872 | tf_op jit(solution)/shard_map/ppermute | solution.py:388
  55.5 13.8 %copy-start = (f32[64,2048]{1,0:T(8,128)S(1)}, f32[64,2048]{1,0:T(8,128)}, u32[]{:S(2)}) copy-start(f32[64,2048]{1,0:T(8,128)} %refs_2_.3) | copy-start | bytes 1572868
  55.5 13.8 %copy-start.1 = (f32[64,2048]{1,0:T(8,128)S(1)}, f32[64,2048]{1,0:T(8,128)}, u32[]{:S(2)}) copy-start(f32[64,2048]{1,0:T(8,128)} %refs_3_.3) | copy-start | bytes 1572868
  55.5 13.8 %copy-start.2 = (f32[64,2048]{1,0:T(8,128)S(1)}, f32[64,2048]{1,0:T(8,128)}, u32[]{:S(2)}) copy-start(f32[64,2048]{1,0:T(8,128)} %refs_4_.3) | copy-start | bytes 1572868
  55.6 9.3 %collective-permute-start.13 = (f32[128,1024]{1,0:T(8,128)S(1)}, f32[128,1024]{1,0:T(8,128)S(1)}, u32[]{:S(2)}, u32[]{:S(2)}) collective-permute-start(f32[128,1024]{1,0:T(8,128)S(1)} %get-tuple-element.47.refs_2_), channel_id=1, source_target_pairs={{0,32},{4,12},{8,40},{12,4},{16,48},{20,28},{24,56},{28,20},{32,0}... | collective-permute-start | bytes 1572872 | tf_op jit(solution)/shard_map/ppermute | solution.py:388
  62.8 6.5 %collective-permute-start.16 = (f32[64,1024]{1,0:T(8,128)S(1)}, f32[64,1024]{1,0:T(8,128)S(1)}, u32[]{:S(2)}, u32[]{:S(2)}) collective-permute-start(f32[64,1024]{1,0:T(8,128)S(1)} %get-tuple-element.49.refs_2_), channel_id=1, source_target_pairs={{0,32},{4,12},{8,40},{12,4},{16,48},{20,28},{24,56},{28,20},{32,0}... | collective-permute-start | bytes 786440 | tf_op jit(solution)/shard_map/ppermute | solution.py:388
  64.9 7.7 %collective-permute-start.15 = (f32[64,1024]{1,0:T(8,128)S(1)}, f32[64,1024]{1,0:T(8,128)S(1)}, u32[]{:S(2)}, u32[]{:S(2)}) collective-permute-start(f32[64,1024]{1,0:T(8,128)S(1)} %get-tuple-element.51.refs_5_), channel_id=1, source_target_pairs={{0,96},{4,28},{8,104},{12,20},{16,112},{20,12},{24,120},{28,4},{32... | collective-permute-start | bytes 786440 | tf_op jit(solution)/shard_map/ppermute | solution.py:388
  73.0 5.9 %collective-permute-start.19 = (f32[8,64]{1,0:T(8,128)S(1)}, f32[8,64]{1,0:T(8,128)S(1)}, u32[]{:S(2)}, u32[]{:S(2)}) collective-permute-start(f32[8,64]{1,0:T(8,128)S(1)} %add.3.refs_0_.refs_4_), channel_id=1, source_target_pairs={{0,2},{1,3},{2,0},{3,1},{4,6},{5,7},{6,4},{7,5},{8,10},{9,11},{10,... | collective-permute-start | bytes 6152 | tf_op jit(solution)/shard_map/ppermute | solution.py:392
  76.9 4.8 %collective-permute-start.18 = (f32[8,64]{1,0:T(8,128)S(1)}, f32[8,64]{1,0:T(8,128)S(1)}, u32[]{:S(2)}, u32[]{:S(2)}) collective-permute-start(f32[8,64]{1,0:T(8,128)S(1)} %add.3.refs_0_.refs_4_), channel_id=1, source_target_pairs={{0,3},{1,2},{2,1},{3,0},{4,7},{5,6},{6,5},{7,4},{8,11},{9,10},{10,... | collective-permute-start | bytes 6152 | tf_op jit(solution)/shard_map/ppermute | solution.py:392
  77.6 4.1 %collective-permute-start.17 = (f32[8,64]{1,0:T(8,128)S(1)}, f32[8,64]{1,0:T(8,128)S(1)}, u32[]{:S(2)}, u32[]{:S(2)}) collective-permute-start(f32[8,64]{1,0:T(8,128)S(1)} %add.3.refs_0_.refs_4_), channel_id=1, source_target_pairs={{0,1},{1,0},{2,3},{3,2},{4,5},{5,4},{6,7},{7,6},{8,9},{9,8},{10,11... | collective-permute-start | bytes 6152 | tf_op jit(solution)/shard_map/ppermute | solution.py:392

commit v4 on v3

--- a/solution.py
+++ b/solution.py
@@ -14,7 +14,7 @@
 ROWS = 64
 TILES = 16
 STRIPS = 8
-FORTH, BACK = (0, 1, 2, 3), (1, 0, 3, 2)
+FORTH, BACK = (0, 1, 3, 2), (1, 0, 2, 3)
 CHAINS = ((0, 0, 768, FORTH), (1, 0, 768, BACK), (0, 768, 256, FORTH), (1, 768, 256, BACK))
 PARTS = [sum(chain[2] for chain in CHAINS if chain[0] == part) for part in (0, 1)]
 ORDER = (

time: 82.7 us -> 81.4 us (0.984)
  waiting for transfers between devices: 28 us -> 24.6 us
  starting transfers between devices: 25.2 us -> 27.3 us
    ppermute x8, waiting for transfers between devices: 20.6 us -> 17.3 us  [on_device(): came[i] = lax.ppermute(last, 'dp', SWAPS[order[step - 1]])]
    ppermute x8, starting transfers between devices: 11 us -> 13.2 us  [on_device(): came[i] = lax.ppermute(last, 'dp', SWAPS[order[step - 1]])]
where the time goes in v4:
time: 81.4 us; the launch traced here: 81.3 us
  Pallas kernels  28.4 us (35%)
  starting transfers between devices  27.3 us (34%)
  waiting for transfers between devices  24.6 us (30%)
  between operations  0.88 us (1%)
    pallas_call x26, Pallas kernels, call(): pl.pallas_call(run, in_specs=specs, cost_estimate=cost, **more)  20.8 us
    ppermute x8, waiting for transfers between devices, on_device(): came[i] = lax.ppermute(last, 'dp', SWAPS[order[step - 1]])  17.3 us
    ppermute x8, starting transfers between devices, on_device(): came[i] = lax.ppermute(last, 'dp', SWAPS[order[step - 1]])  13.2 us
    ppermute x4, starting transfers between devices, on_device(): came[i] = lax.ppermute(last, 'dp', SWAPS[order[0]])  7.7 us
    pallas_call x1, Pallas kernels, prep(): pl.pallas_call(functools.partial(prep_kernel, pieces), out_shape=(VMEM((2...  6.73 us
    ppermute x3, starting transfers between devices, on_device(): sums = [sums] + [lax.ppermute(sums, 'tensor', swap) for swap in Z_SWAPS]  4.89 us
    ppermute x4, waiting for transfers between devices, on_device(): came[i] = lax.ppermute(last, 'dp', SWAPS[order[0]])  2.89 us
    ppermute x3, waiting for transfers between devices, on_device(): sums = [sums] + [lax.ppermute(sums, 'tensor', swap) for swap in Z_SWAPS]  2.78 us
  transfers between devices with their start and end apart: 20, of which 9 were waited for; matrix products, arithmetic and copies ran while one was open for 0% of the time, Pallas kernels for 25%

profile of v4, /device:TPU:0, one launch (start us, length us, event | category | flops | bytes accessed | tf_op | source)
XLA Modules:
  0.0 81.3 jit_solution(7391622418981015407)
XLA Ops:
  0.6 6.7 %prep.1 = (bf16[32,64,2048]{2,1,0:T(8,128)(2,1)S(1)}, bf16[2048,1024]{1,0:T(8,128)(2,1)S(1)}, bf16[2048,1024]{1,0:T(8,128)(2,1)S(1)}, f32[512,768]{1,0:T(8,128)S(1)}) custom-call(bf16[2048,2048]{1,0:T(8,128)(2,1)} %out_grad.1, bf16[2048,2048]{1,0:T(8,128)(2,1)} %inputs.1), custom_call_target="tpu_custom_call" | custom-call | tf_op jit(solution)/shard_map/prep/pallas_call | solution.py:120
  7.5 1.8 %s1_1.1.refs_3_ = f32[512,768]{1,0:T(8,128)S(1)} custom-call(bf16[32,64,2048]{2,1,0:T(8,128)(2,1)S(1)} %get-tuple-element.33.refs_0_, bf16[2048,1024]{1,0:T(8,128)(2,1)S(1)} %get-tuple-element.34.refs_1_, bf16[2048,1024]{1,0:T(8,128)(2,1)S(1)} %get-tuple-element.35.refs_2_, f32[512,768]{1,0:T(8,128)S(1)} %get-tuple-element.36.refs_3_), custom_call_target="tpu_custom_call" | custom-call | flops 1 | bytes 1 | tf_op jit(solution)/shard_map/s1_1/pallas_call | solution.py:142
  9.8 1.8 %oq_0.1.refs_0_.refs_2_ = f32[512,768]{1,0:T(8,128)S(1)} custom-call(bf16[32,64,2048]{2,1,0:T(8,128)(2,1)S(1)} %get-tuple-element.33.refs_0_, bf16[2048,1024]{1,0:T(8,128)(2,1)S(1)} %get-tuple-element.34.refs_1_, bf16[2048,1024]{1,0:T(8,128)(2,1)S(1)} %get-tuple-element.35.refs_2_, f32[512,768]{1,0:T(8,128)S(1)} %s1_1.1.refs_3_), custom_call_target="tpu_custom_call" | custom-call | flops 1 | bytes 1 | tf_op jit(solution)/shard_map/oq_0/pallas_call | solution.py:142
  11.8 1.7 %collective-permute-start.2 = (f32[512,768]{1,0:T(8,128)S(1)}, f32[512,768]{1,0:T(8,128)S(1)}, u32[]{:S(2)}, u32[]{:S(2)}) collective-permute-start(f32[512,768]{1,0:T(8,128)S(1)} %a1_0.1.refs_4_), channel_id=1, source_target_pairs={{0,8},{4,36},{8,0},{12,44},{16,24},{20,52},{24,16},{28,60},{32,40}... | collective-permute-start | bytes 4718600 | tf_op jit(solution)/shard_map/ppermute | solution.py:373
  13.5 1.8 %o1_1.1.refs_3_ = f32[512,768]{1,0:T(8,128)S(1)} custom-call(bf16[32,64,2048]{2,1,0:T(8,128)(2,1)S(1)} %get-tuple-element.33.refs_0_, bf16[2048,1024]{1,0:T(8,128)(2,1)S(1)} %get-tuple-element.34.refs_1_, bf16[2048,1024]{1,0:T(8,128)(2,1)S(1)} %get-tuple-element.35.refs_2_, f32[512,768]{1,0:T(8,128)S(1)} %collective-permute-done.refs_3_, ...), custom_call_target="tpu_custom_call" | custom-call | flops 1 | bytes 1 | tf_op jit(solution)/shard_map/o1_1/pallas_call | solution.py:142
  15.3 2.6 %collective-permute-start.5 = (f32[512,768]{1,0:T(8,128)S(1)}, f32[512,768]{1,0:T(8,128)S(1)}, u32[]{:S(2)}, u32[]{:S(2)}) collective-permute-start(f32[512,768]{1,0:T(8,128)S(1)} %o1_1.1.refs_3_), channel_id=1, source_target_pairs={{0,24},{4,100},{8,16},{12,108},{16,8},{20,116},{24,0},{28,124},{32... | collective-permute-start | bytes 4718600 | tf_op jit(solution)/shard_map/ppermute | solution.py:368
  17.8 3.4 %s0_01.1.refs_3_ = f32[1024,768]{1,0:T(8,128)S(1)} custom-call(bf16[32,64,2048]{2,1,0:T(8,128)(2,1)S(1)} %get-tuple-element.33.refs_0_, bf16[2048,1024]{1,0:T(8,128)(2,1)S(1)} %get-tuple-element.34.refs_1_, bf16[2048,1024]{1,0:T(8,128)(2,1)S(1)} %get-tuple-element.35.refs_2_, f32[512,768]{1,0:T(8,128)S(1)} %o1_1.1.refs_3_), custom_call_target="tpu_custom_call" | custom-call | flops 1 | bytes 1 | tf_op jit(solution)/shard_map/s0_01/pallas_call | solution.py:142
  23.3 1.8 %op_0.1.refs_3_.refs_0_ = f32[512,768]{1,0:T(8,128)S(1)} custom-call(bf16[32,64,2048]{2,1,0:T(8,128)(2,1)S(1)} %get-tuple-element.33.refs_0_, bf16[2048,1024]{1,0:T(8,128)(2,1)S(1)} %get-tuple-element.34.refs_1_, bf16[2048,1024]{1,0:T(8,128)(2,1)S(1)} %get-tuple-element.35.refs_2_, f32[1024,256]{1,0:T(8,128)S(1)} %s1_23.1.refs_3_), custom_call_target="tpu_custom_call" | custom-call | flops 1 | bytes 1 | tf_op jit(solution)/shard_map/op_0/pallas_call | solution.py:142
  25.1 1.8 %op_1.1.refs_4_.refs_0_ = f32[512,768]{1,0:T(8,128)S(1)} custom-call(bf16[32,64,2048]{2,1,0:T(8,128)(2,1)S(1)} %get-tuple-element.33.refs_0_, bf16[2048,1024]{1,0:T(8,128)(2,1)S(1)} %get-tuple-element.34.refs_1_, bf16[2048,1024]{1,0:T(8,128)(2,1)S(1)} %get-tuple-element.35.refs_2_, f32[512,768]{1,0:T(8,128)S(1)} %op_0.1.refs_3_.refs_0_), custom_call_target="tpu_custom_call" | custom-call | flops 1 | bytes 1 | tf_op jit(solution)/shard_map/op_1/pallas_call | solution.py:142
  26.9 1.7 %collective-permute-done.3.refs_3_ = f32[1024,256]{1,0:T(8,128)S(1)} collective-permute-done((f32[1024,256]{1,0:T(8,128)S(1)}, f32[1024,256]{1,0:T(8,128)S(1)}, u32[]{:S(2)}, u32[]{:S(2)}) %collective-permute-start.3) | collective-permute-done | bytes 1048608 | tf_op jit(solution)/shard_map/ppermute | solution.py:352
  29.4 1.3 %collective-permute-start.8 = (f32[512,256]{1,0:T(8,128)S(1)}, f32[512,256]{1,0:T(8,128)S(1)}, u32[]{:S(2)}, u32[]{:S(2)}) collective-permute-start(f32[512,256]{1,0:T(8,128)S(1)} %o1_2.1.refs_4_), channel_id=1, source_target_pairs={{0,8},{4,36},{8,0},{12,44},{16,24},{20,52},{24,16},{28,60},{32,40}... | collective-permute-start | bytes 1572872 | tf_op jit(solution)/shard_map/ppermute | solution.py:368
  31.4 2.2 %collective-permute-start.9 = (f32[512,256]{1,0:T(8,128)S(1)}, f32[512,256]{1,0:T(8,128)S(1)}, u32[]{:S(2)}, u32[]{:S(2)}) collective-permute-start(f32[512,256]{1,0:T(8,128)S(1)} %o1_3.1.refs_3_), channel_id=1, source_target_pairs={{0,24},{4,100},{8,16},{12,108},{16,8},{20,116},{24,0},{28,124},{32... | collective-permute-start | bytes 1572872 | tf_op jit(solution)/shard_map/ppermute | solution.py:368
  35.1 1.9 %collective-permute-done.5.refs_1_ = f32[512,768]{1,0:T(8,128)S(1)} collective-permute-done((f32[512,768]{1,0:T(8,128)S(1)}, f32[512,768]{1,0:T(8,128)S(1)}, u32[]{:S(2)}, u32[]{:S(2)}) %collective-permute-start.5) | collective-permute-done | bytes 1572896 | tf_op jit(solution)/shard_map/ppermute | solution.py:368
  37.6 2.6 %collective-permute-start.6 = (f32[256,768]{1,0:T(8,128)S(1)}, f32[256,768]{1,0:T(8,128)S(1)}, u32[]{:S(2)}, u32[]{:S(2)}) collective-permute-start(f32[256,768]{1,0:T(8,128)S(1)} %get-tuple-element.39.refs_4_), channel_id=1, source_target_pairs={{0,24},{4,100},{8,16},{12,108},{16,8},{20,116},{24,0},{28,124},{32... | collective-permute-start | bytes 2359304 | tf_op jit(solution)/shard_map/ppermute | solution.py:388
  43.2 2.2 %collective-permute-start.10 = (f32[256,256]{1,0:T(8,128)S(1)}, f32[256,256]{1,0:T(8,128)S(1)}, u32[]{:S(2)}, u32[]{:S(2)}) collective-permute-start(f32[256,256]{1,0:T(8,128)S(1)} %get-tuple-element.42.refs_4_), channel_id=1, source_target_pairs={{0,24},{4,100},{8,16},{12,108},{16,8},{20,116},{24,0},{28,124},{32... | collective-permute-start | bytes 786440 | tf_op jit(solution)/shard_map/ppermute | solution.py:388
  45.4 6.8 %collective-permute-done.12.refs_3_ = f32[256,256]{1,0:T(8,128)S(1)} collective-permute-done((f32[256,256]{1,0:T(8,128)S(1)}, f32[256,256]{1,0:T(8,128)S(1)}, u32[]{:S(2)}, u32[]{:S(2)}) %collective-permute-start.12) | collective-permute-done | bytes 262176 | tf_op jit(solution)/shard_map/ppermute | solution.py:388
  52.3 1.8 %collective-permute-start.14 = (f32[128,1024]{1,0:T(8,128)S(1)}, f32[128,1024]{1,0:T(8,128)S(1)}, u32[]{:S(2)}, u32[]{:S(2)}) collective-permute-start(f32[128,1024]{1,0:T(8,128)S(1)} %get-tuple-element.45.refs_4_), channel_id=1, source_target_pairs={{0,32},{4,12},{8,40},{12,4},{16,48},{20,28},{24,56},{28,20},{32,0}... | collective-permute-start | bytes 1572872 | tf_op jit(solution)/shard_map/ppermute | solution.py:388
  54.3 2.8 %collective-permute-start.13 = (f32[128,1024]{1,0:T(8,128)S(1)}, f32[128,1024]{1,0:T(8,128)S(1)}, u32[]{:S(2)}, u32[]{:S(2)}) collective-permute-start(f32[128,1024]{1,0:T(8,128)S(1)} %get-tuple-element.47.refs_2_), channel_id=1, source_target_pairs={{0,96},{4,28},{8,104},{12,20},{16,112},{20,12},{24,120},{28,4},{32... | collective-permute-start | bytes 1572872 | tf_op jit(solution)/shard_map/ppermute | solution.py:388
  57.1 4.5 %collective-permute-done.14.refs_1_ = f32[128,1024]{1,0:T(8,128)S(1)} collective-permute-done((f32[128,1024]{1,0:T(8,128)S(1)}, f32[128,1024]{1,0:T(8,128)S(1)}, u32[]{:S(2)}, u32[]{:S(2)}) %collective-permute-start.14) | collective-permute-done | bytes 524320 | tf_op jit(solution)/shard_map/ppermute | solution.py:388
  61.6 3.1 %collective-permute-start.16 = (f32[64,1024]{1,0:T(8,128)S(1)}, f32[64,1024]{1,0:T(8,128)S(1)}, u32[]{:S(2)}, u32[]{:S(2)}) collective-permute-start(f32[64,1024]{1,0:T(8,128)S(1)} %get-tuple-element.49.refs_2_), channel_id=1, source_target_pairs={{0,96},{4,28},{8,104},{12,20},{16,112},{20,12},{24,120},{28,4},{32... | collective-permute-start | bytes 786440 | tf_op jit(solution)/shard_map/ppermute | solution.py:388
  65.0 4.3 %collective-permute-done.16.refs_1_ = f32[64,1024]{1,0:T(8,128)S(1)} collective-permute-done((f32[64,1024]{1,0:T(8,128)S(1)}, f32[64,1024]{1,0:T(8,128)S(1)}, u32[]{:S(2)}, u32[]{:S(2)}) %collective-permute-start.16) | collective-permute-done | bytes 262176 | tf_op jit(solution)/shard_map/ppermute | solution.py:388
  69.7 1.6 %collective-permute-done.15.refs_1_ = f32[64,1024]{1,0:T(8,128)S(1)} collective-permute-done((f32[64,1024]{1,0:T(8,128)S(1)}, f32[64,1024]{1,0:T(8,128)S(1)}, u32[]{:S(2)}, u32[]{:S(2)}) %collective-permute-start.15) | collective-permute-done | bytes 262176 | tf_op jit(solution)/shard_map/ppermute | solution.py:388
  71.7 3.9 %collective-permute-start.19 = (f32[8,64]{1,0:T(8,128)S(1)}, f32[8,64]{1,0:T(8,128)S(1)}, u32[]{:S(2)}, u32[]{:S(2)}) collective-permute-start(f32[8,64]{1,0:T(8,128)S(1)} %add.3.refs_0_.refs_4_), channel_id=1, source_target_pairs={{0,2},{1,3},{2,0},{3,1},{4,6},{5,7},{6,4},{7,5},{8,10},{9,11},{10,... | collective-permute-start | bytes 6152 | tf_op jit(solution)/shard_map/ppermute | solution.py:392
  77.7 2.8 %collective-permute-done.18.refs_2_ = f32[8,64]{1,0:T(8,128)S(1)} collective-permute-done((f32[8,64]{1,0:T(8,128)S(1)}, f32[8,64]{1,0:T(8,128)S(1)}, u32[]{:S(2)}, u32[]{:S(2)}) %collective-permute-start.18) | collective-permute-done | bytes 2080 | tf_op jit(solution)/shard_map/ppermute | solution.py:392
  (51 shorter events, 13.8 us)
Async XLA Ops:
  7.4 4.3 %collective-permute-start.1 = (f32[512,768]{1,0:T(8,128)S(1)}, f32[512,768]{1,0:T(8,128)S(1)}, u32[]{:S(2)}, u32[]{:S(2)}) collective-permute-start(f32[512,768]{1,0:T(8,128)S(1)} %get-tuple-element.36.refs_3_), channel_id=1, source_target_pairs={{0,4},{4,0},{8,12},{12,8},{16,20},{20,16},{24,28},{28,24},{32,36},... | collective-permute-start | bytes 4718600 | tf_op jit(solution)/shard_map/ppermute | solution.py:352
  9.3 4.2 %collective-permute-start = (f32[512,768]{1,0:T(8,128)S(1)}, f32[512,768]{1,0:T(8,128)S(1)}, u32[]{:S(2)}, u32[]{:S(2)}) collective-permute-start(f32[512,768]{1,0:T(8,128)S(1)} %s1_1.1.refs_3_), channel_id=1, source_target_pairs={{0,4},{4,0},{8,12},{12,8},{16,20},{20,16},{24,28},{28,24},{32,36},... | collective-permute-start | bytes 4718600 | tf_op jit(solution)/shard_map/ppermute | solution.py:352
  11.8 23.0 %collective-permute-start.2 = (f32[512,768]{1,0:T(8,128)S(1)}, f32[512,768]{1,0:T(8,128)S(1)}, u32[]{:S(2)}, u32[]{:S(2)}) collective-permute-start(f32[512,768]{1,0:T(8,128)S(1)} %a1_0.1.refs_4_), channel_id=1, source_target_pairs={{0,8},{4,36},{8,0},{12,44},{16,24},{20,52},{24,16},{28,60},{32,40}... | collective-permute-start | bytes 4718600 | tf_op jit(solution)/shard_map/ppermute | solution.py:373
  15.3 21.7 %collective-permute-start.5 = (f32[512,768]{1,0:T(8,128)S(1)}, f32[512,768]{1,0:T(8,128)S(1)}, u32[]{:S(2)}, u32[]{:S(2)}) collective-permute-start(f32[512,768]{1,0:T(8,128)S(1)} %o1_1.1.refs_3_), channel_id=1, source_target_pairs={{0,24},{4,100},{8,16},{12,108},{16,8},{20,116},{24,0},{28,124},{32... | collective-permute-start | bytes 4718600 | tf_op jit(solution)/shard_map/ppermute | solution.py:368
  21.2 15.9 %collective-permute-start.4 = (f32[1024,768]{1,0:T(8,128)S(1)}, f32[1024,768]{1,0:T(8,128)S(1)}, u32[]{:S(2)}, u32[]{:S(2)}) collective-permute-start(f32[1024,768]{1,0:T(8,128)S(1)} %s0_01.1.refs_3_), channel_id=1, source_target_pairs={{0,4},{4,0},{8,12},{12,8},{16,20},{20,16},{24,28},{28,24},{32,36},... | collective-permute-start | bytes 9437192 | tf_op jit(solution)/shard_map/ppermute | solution.py:352
  22.9 5.8 %collective-permute-start.3 = (f32[1024,256]{1,0:T(8,128)S(1)}, f32[1024,256]{1,0:T(8,128)S(1)}, u32[]{:S(2)}, u32[]{:S(2)}) collective-permute-start(f32[1024,256]{1,0:T(8,128)S(1)} %s1_23.1.refs_3_), channel_id=1, source_target_pairs={{0,4},{4,0},{8,12},{12,8},{16,20},{20,16},{24,28},{28,24},{32,36},... | collective-permute-start | bytes 3145736 | tf_op jit(solution)/shard_map/ppermute | solution.py:352
  29.4 13.8 %collective-permute-start.8 = (f32[512,256]{1,0:T(8,128)S(1)}, f32[512,256]{1,0:T(8,128)S(1)}, u32[]{:S(2)}, u32[]{:S(2)}) collective-permute-start(f32[512,256]{1,0:T(8,128)S(1)} %o1_2.1.refs_4_), channel_id=1, source_target_pairs={{0,8},{4,36},{8,0},{12,44},{16,24},{20,52},{24,16},{28,60},{32,40}... | collective-permute-start | bytes 1572872 | tf_op jit(solution)/shard_map/ppermute | solution.py:368
  31.4 11.2 %collective-permute-start.9 = (f32[512,256]{1,0:T(8,128)S(1)}, f32[512,256]{1,0:T(8,128)S(1)}, u32[]{:S(2)}, u32[]{:S(2)}) collective-permute-start(f32[512,256]{1,0:T(8,128)S(1)} %o1_3.1.refs_3_), channel_id=1, source_target_pairs={{0,24},{4,100},{8,16},{12,108},{16,8},{20,116},{24,0},{28,124},{32... | collective-permute-start | bytes 1572872 | tf_op jit(solution)/shard_map/ppermute | solution.py:368
  34.8 5.3 %collective-permute-start.7 = (f32[1024,256]{1,0:T(8,128)S(1)}, f32[1024,256]{1,0:T(8,128)S(1)}, u32[]{:S(2)}, u32[]{:S(2)}) collective-permute-start(f32[1024,256]{1,0:T(8,128)S(1)} %s0_23.1.refs_2_), channel_id=1, source_target_pairs={{0,4},{4,0},{8,12},{12,8},{16,20},{20,16},{24,28},{28,24},{32,36},... | collective-permute-start | bytes 3145736 | tf_op jit(solution)/shard_map/ppermute | solution.py:352
  37.3 14.9 %collective-permute-start.11 = (f32[256,768]{1,0:T(8,128)S(1)}, f32[256,768]{1,0:T(8,128)S(1)}, u32[]{:S(2)}, u32[]{:S(2)}) collective-permute-start(f32[256,768]{1,0:T(8,128)S(1)} %get-tuple-element.37.refs_2_), channel_id=1, source_target_pairs={{0,8},{4,36},{8,0},{12,44},{16,24},{20,52},{24,16},{28,60},{32,40}... | collective-permute-start | bytes 2359304 | tf_op jit(solution)/shard_map/ppermute | solution.py:388
  37.6 16.6 %collective-permute-start.6 = (f32[256,768]{1,0:T(8,128)S(1)}, f32[256,768]{1,0:T(8,128)S(1)}, u32[]{:S(2)}, u32[]{:S(2)}) collective-permute-start(f32[256,768]{1,0:T(8,128)S(1)} %get-tuple-element.39.refs_4_), channel_id=1, source_target_pairs={{0,24},{4,100},{8,16},{12,108},{16,8},{20,116},{24,0},{28,124},{32... | collective-permute-start | bytes 2359304 | tf_op jit(solution)/shard_map/ppermute | solution.py:388
  42.6 9.5 %collective-permute-start.12 = (f32[256,256]{1,0:T(8,128)S(1)}, f32[256,256]{1,0:T(8,128)S(1)}, u32[]{:S(2)}, u32[]{:S(2)}) collective-permute-start(f32[256,256]{1,0:T(8,128)S(1)} %get-tuple-element.40.refs_2_), channel_id=1, source_target_pairs={{0,8},{4,36},{8,0},{12,44},{16,24},{20,52},{24,16},{28,60},{32,40}... | collective-permute-start | bytes 786440 | tf_op jit(solution)/shard_map/ppermute | solution.py:388
  43.2 11.0 %collective-permute-start.10 = (f32[256,256]{1,0:T(8,128)S(1)}, f32[256,256]{1,0:T(8,128)S(1)}, u32[]{:S(2)}, u32[]{:S(2)}) collective-permute-start(f32[256,256]{1,0:T(8,128)S(1)} %get-tuple-element.42.refs_4_), channel_id=1, source_target_pairs={{0,24},{4,100},{8,16},{12,108},{16,8},{20,116},{24,0},{28,124},{32... | collective-permute-start | bytes 786440 | tf_op jit(solution)/shard_map/ppermute | solution.py:388
  52.3 9.3 %collective-permute-start.14 = (f32[128,1024]{1,0:T(8,128)S(1)}, f32[128,1024]{1,0:T(8,128)S(1)}, u32[]{:S(2)}, u32[]{:S(2)}) collective-permute-start(f32[128,1024]{1,0:T(8,128)S(1)} %get-tuple-element.45.refs_4_), channel_id=1, source_target_pairs={{0,32},{4,12},{8,40},{12,4},{16,48},{20,28},{24,56},{28,20},{32,0}... | collective-permute-start | bytes 1572872 | tf_op jit(solution)/shard_map/ppermute | solution.py:388
  54.3 15.0 %copy-start = (f32[64,2048]{1,0:T(8,128)S(1)}, f32[64,2048]{1,0:T(8,128)}, u32[]{:S(2)}) copy-start(f32[64,2048]{1,0:T(8,128)} %refs_2_.3) | copy-start | bytes 1572868
  54.3 15.0 %copy-start.1 = (f32[64,2048]{1,0:T(8,128)S(1)}, f32[64,2048]{1,0:T(8,128)}, u32[]{:S(2)}) copy-start(f32[64,2048]{1,0:T(8,128)} %refs_3_.3) | copy-start | bytes 1572868
  54.3 15.0 %copy-start.2 = (f32[64,2048]{1,0:T(8,128)S(1)}, f32[64,2048]{1,0:T(8,128)}, u32[]{:S(2)}) copy-start(f32[64,2048]{1,0:T(8,128)} %refs_4_.3) | copy-start | bytes 1572868
  54.3 10.5 %collective-permute-start.13 = (f32[128,1024]{1,0:T(8,128)S(1)}, f32[128,1024]{1,0:T(8,128)S(1)}, u32[]{:S(2)}, u32[]{:S(2)}) collective-permute-start(f32[128,1024]{1,0:T(8,128)S(1)} %get-tuple-element.47.refs_2_), channel_id=1, source_target_pairs={{0,96},{4,28},{8,104},{12,20},{16,112},{20,12},{24,120},{28,4},{32... | collective-permute-start | bytes 1572872 | tf_op jit(solution)/shard_map/ppermute | solution.py:388
  61.6 7.7 %collective-permute-start.16 = (f32[64,1024]{1,0:T(8,128)S(1)}, f32[64,1024]{1,0:T(8,128)S(1)}, u32[]{:S(2)}, u32[]{:S(2)}) collective-permute-start(f32[64,1024]{1,0:T(8,128)S(1)} %get-tuple-element.49.refs_2_), channel_id=1, source_target_pairs={{0,96},{4,28},{8,104},{12,20},{16,112},{20,12},{24,120},{28,4},{32... | collective-permute-start | bytes 786440 | tf_op jit(solution)/shard_map/ppermute | solution.py:388
  64.8 6.5 %collective-permute-start.15 = (f32[64,1024]{1,0:T(8,128)S(1)}, f32[64,1024]{1,0:T(8,128)S(1)}, u32[]{:S(2)}, u32[]{:S(2)}) collective-permute-start(f32[64,1024]{1,0:T(8,128)S(1)} %get-tuple-element.51.refs_5_), channel_id=1, source_target_pairs={{0,32},{4,12},{8,40},{12,4},{16,48},{20,28},{24,56},{28,20},{32,0}... | collective-permute-start | bytes 786440 | tf_op jit(solution)/shard_map/ppermute | solution.py:388
  71.7 5.9 %collective-permute-start.19 = (f32[8,64]{1,0:T(8,128)S(1)}, f32[8,64]{1,0:T(8,128)S(1)}, u32[]{:S(2)}, u32[]{:S(2)}) collective-permute-start(f32[8,64]{1,0:T(8,128)S(1)} %add.3.refs_0_.refs_4_), channel_id=1, source_target_pairs={{0,2},{1,3},{2,0},{3,1},{4,6},{5,7},{6,4},{7,5},{8,10},{9,11},{10,... | collective-permute-start | bytes 6152 | tf_op jit(solution)/shard_map/ppermute | solution.py:392
  75.6 4.8 %collective-permute-start.18 = (f32[8,64]{1,0:T(8,128)S(1)}, f32[8,64]{1,0:T(8,128)S(1)}, u32[]{:S(2)}, u32[]{:S(2)}) collective-permute-start(f32[8,64]{1,0:T(8,128)S(1)} %add.3.refs_0_.refs_4_), channel_id=1, source_target_pairs={{0,3},{1,2},{2,1},{3,0},{4,7},{5,6},{6,5},{7,4},{8,11},{9,10},{10,... | collective-permute-start | bytes 6152 | tf_op jit(solution)/shard_map/ppermute | solution.py:392
  76.3 4.1 %collective-permute-start.17 = (f32[8,64]{1,0:T(8,128)S(1)}, f32[8,64]{1,0:T(8,128)S(1)}, u32[]{:S(2)}, u32[]{:S(2)}) collective-permute-start(f32[8,64]{1,0:T(8,128)S(1)} %add.3.refs_0_.refs_4_), channel_id=1, source_target_pairs={{0,1},{1,0},{2,3},{3,2},{4,5},{5,4},{6,7},{7,6},{8,9},{9,8},{10,11... | collective-permute-start | bytes 6152 | tf_op jit(solution)/shard_map/ppermute | solution.py:392

commit v5 on v4

--- a/solution.py
+++ b/solution.py
@@ -63,13 +63,13 @@
     return high ^ (i & 1), high
 
 
-def half_copies(inputs, half, which, arrived, first):
-    rows, width = half.shape[0] // STRIPS, half.shape[1]
-    first_col = which * (inputs.shape[1] - width)
+def half_copies(inputs, half, which, arrived, first, lo, hi):
+    rows = half.shape[0] // STRIPS
+    first_col = which * (inputs.shape[1] - half.shape[1])
     return [
         pltpu.make_async_copy(
-            inputs.at[k * rows : (k + 1) * rows, first_col : first_col + width],
-            half.at[k * rows : (k + 1) * rows],
+            inputs.at[k * rows : (k + 1) * rows, first_col + lo : first_col + hi],
+            half.at[k * rows : (k + 1) * rows, lo:hi],
             arrived.at[first + k],
         )
         for k in range(STRIPS)
@@ -86,8 +86,10 @@
         )
         for k in range(strips)
     ]
-    copies += half_copies(inputs, left, 0, arrived, strips)
-    copies += half_copies(inputs, right, 1, arrived, strips + STRIPS)
+    cut = pieces[0][3]
+    copies += half_copies(inputs, left, 0, arrived, strips, 0, cut)
+    copies += half_copies(inputs, right, 1, arrived, strips + STRIPS, 0, right.shape[1])
+    copies += half_copies(inputs, left, 0, arrived, strips + 2 * STRIPS, cut, left.shape[1])
     for copy in copies:
         copy.start()
     me = lax.axis_index("dp")
@@ -124,7 +126,7 @@
         out_specs=[in_vmem()] * 4,
         scratch_shapes=[
             VMEM((strips, tokens, rows // strips), BF16),
-            pltpu.SemaphoreType.DMA((strips + 2 * STRIPS,)),
+            pltpu.SemaphoreType.DMA((strips + 3 * STRIPS,)),
         ],
         compiler_params=params(12),
         name="prep",

time: 81.4 us -> 81.2 us (level)
  no operation moved by 1% of the time
where the time goes in v5:
time: 81.2 us; the launch traced here: 81.1 us
  Pallas kernels  28.2 us (35%)
  starting transfers between devices  27.4 us (34%)
  waiting for transfers between devices  24.6 us (30%)
  between operations  0.87 us (1%)
    pallas_call x26, Pallas kernels, call(): pl.pallas_call(run, in_specs=specs, cost_estimate=cost, **more)  20.8 us
    ppermute x8, waiting for transfers between devices, on_device(): came[i] = lax.ppermute(last, 'dp', SWAPS[order[step - 1]])  17.2 us
    ppermute x8, starting transfers between devices, on_device(): came[i] = lax.ppermute(last, 'dp', SWAPS[order[step - 1]])  13.2 us
    ppermute x4, starting transfers between devices, on_device(): came[i] = lax.ppermute(last, 'dp', SWAPS[order[0]])  7.69 us
    pallas_call x1, Pallas kernels, prep(): pl.pallas_call(functools.partial(prep_kernel, pieces), out_shape=(VMEM((2...  6.52 us
    ppermute x3, starting transfers between devices, on_device(): sums = [sums] + [lax.ppermute(sums, 'tensor', swap) for swap in Z_SWAPS]  4.89 us
    ppermute x4, waiting for transfers between devices, on_device(): came[i] = lax.ppermute(last, 'dp', SWAPS[order[0]])  2.9 us
    ppermute x3, waiting for transfers between devices, on_device(): sums = [sums] + [lax.ppermute(sums, 'tensor', swap) for swap in Z_SWAPS]  2.78 us
  transfers between devices with their start and end apart: 20, of which 9 were waited for; matrix products, arithmetic and copies ran while one was open for 0% of the time, Pallas kernels for 25%

profile of v5, /device:TPU:0, one launch (start us, length us, event | category | flops | bytes accessed | tf_op | source)
XLA Modules:
  0.0 81.1 jit_solution(4512219895702777197)
XLA Ops:
  0.6 6.5 %prep.1 = (bf16[32,64,2048]{2,1,0:T(8,128)(2,1)S(1)}, bf16[2048,1024]{1,0:T(8,128)(2,1)S(1)}, bf16[2048,1024]{1,0:T(8,128)(2,1)S(1)}, f32[512,768]{1,0:T(8,128)S(1)}) custom-call(bf16[2048,2048]{1,0:T(8,128)(2,1)} %out_grad.1, bf16[2048,2048]{1,0:T(8,128)(2,1)} %inputs.1), custom_call_target="tpu_custom_call" | custom-call | tf_op jit(solution)/shard_map/prep/pallas_call | solution.py:122
  7.2 1.8 %s1_1.1.refs_3_ = f32[512,768]{1,0:T(8,128)S(1)} custom-call(bf16[32,64,2048]{2,1,0:T(8,128)(2,1)S(1)} %get-tuple-element.33.refs_0_, bf16[2048,1024]{1,0:T(8,128)(2,1)S(1)} %get-tuple-element.34.refs_1_, bf16[2048,1024]{1,0:T(8,128)(2,1)S(1)} %get-tuple-element.35.refs_2_, f32[512,768]{1,0:T(8,128)S(1)} %get-tuple-element.36.refs_3_), custom_call_target="tpu_custom_call" | custom-call | flops 1 | bytes 1 | tf_op jit(solution)/shard_map/s1_1/pallas_call | solution.py:144
  9.6 1.8 %oq_0.1.refs_0_.refs_2_ = f32[512,768]{1,0:T(8,128)S(1)} custom-call(bf16[32,64,2048]{2,1,0:T(8,128)(2,1)S(1)} %get-tuple-element.33.refs_0_, bf16[2048,1024]{1,0:T(8,128)(2,1)S(1)} %get-tuple-element.34.refs_1_, bf16[2048,1024]{1,0:T(8,128)(2,1)S(1)} %get-tuple-element.35.refs_2_, f32[512,768]{1,0:T(8,128)S(1)} %s1_1.1.refs_3_), custom_call_target="tpu_custom_call" | custom-call | flops 1 | bytes 1 | tf_op jit(solution)/shard_map/oq_0/pallas_call | solution.py:144
  11.6 1.7 %collective-permute-start.2 = (f32[512,768]{1,0:T(8,128)S(1)}, f32[512,768]{1,0:T(8,128)S(1)}, u32[]{:S(2)}, u32[]{:S(2)}) collective-permute-start(f32[512,768]{1,0:T(8,128)S(1)} %a1_0.1.refs_4_), channel_id=1, source_target_pairs={{0,8},{4,36},{8,0},{12,44},{16,24},{20,52},{24,16},{28,60},{32,40}... | collective-permute-start | bytes 4718600 | tf_op jit(solution)/shard_map/ppermute | solution.py:375
  13.3 1.8 %o1_1.1.refs_3_ = f32[512,768]{1,0:T(8,128)S(1)} custom-call(bf16[32,64,2048]{2,1,0:T(8,128)(2,1)S(1)} %get-tuple-element.33.refs_0_, bf16[2048,1024]{1,0:T(8,128)(2,1)S(1)} %get-tuple-element.34.refs_1_, bf16[2048,1024]{1,0:T(8,128)(2,1)S(1)} %get-tuple-element.35.refs_2_, f32[512,768]{1,0:T(8,128)S(1)} %collective-permute-done.refs_3_, ...), custom_call_target="tpu_custom_call" | custom-call | flops 1 | bytes 1 | tf_op jit(solution)/shard_map/o1_1/pallas_call | solution.py:144
  15.1 2.6 %collective-permute-start.5 = (f32[512,768]{1,0:T(8,128)S(1)}, f32[512,768]{1,0:T(8,128)S(1)}, u32[]{:S(2)}, u32[]{:S(2)}) collective-permute-start(f32[512,768]{1,0:T(8,128)S(1)} %o1_1.1.refs_3_), channel_id=1, source_target_pairs={{0,24},{4,100},{8,16},{12,108},{16,8},{20,116},{24,0},{28,124},{32... | collective-permute-start | bytes 4718600 | tf_op jit(solution)/shard_map/ppermute | solution.py:370
  17.6 3.4 %s0_01.1.refs_3_ = f32[1024,768]{1,0:T(8,128)S(1)} custom-call(bf16[32,64,2048]{2,1,0:T(8,128)(2,1)S(1)} %get-tuple-element.33.refs_0_, bf16[2048,1024]{1,0:T(8,128)(2,1)S(1)} %get-tuple-element.34.refs_1_, bf16[2048,1024]{1,0:T(8,128)(2,1)S(1)} %get-tuple-element.35.refs_2_, f32[512,768]{1,0:T(8,128)S(1)} %o1_1.1.refs_3_), custom_call_target="tpu_custom_call" | custom-call | flops 1 | bytes 1 | tf_op jit(solution)/shard_map/s0_01/pallas_call | solution.py:144
  23.1 1.8 %op_0.1.refs_3_.refs_0_ = f32[512,768]{1,0:T(8,128)S(1)} custom-call(bf16[32,64,2048]{2,1,0:T(8,128)(2,1)S(1)} %get-tuple-element.33.refs_0_, bf16[2048,1024]{1,0:T(8,128)(2,1)S(1)} %get-tuple-element.34.refs_1_, bf16[2048,1024]{1,0:T(8,128)(2,1)S(1)} %get-tuple-element.35.refs_2_, f32[1024,256]{1,0:T(8,128)S(1)} %s1_23.1.refs_3_), custom_call_target="tpu_custom_call" | custom-call | flops 1 | bytes 1 | tf_op jit(solution)/shard_map/op_0/pallas_call | solution.py:144
  24.9 1.8 %op_1.1.refs_4_.refs_0_ = f32[512,768]{1,0:T(8,128)S(1)} custom-call(bf16[32,64,2048]{2,1,0:T(8,128)(2,1)S(1)} %get-tuple-element.33.refs_0_, bf16[2048,1024]{1,0:T(8,128)(2,1)S(1)} %get-tuple-element.34.refs_1_, bf16[2048,1024]{1,0:T(8,128)(2,1)S(1)} %get-tuple-element.35.refs_2_, f32[512,768]{1,0:T(8,128)S(1)} %op_0.1.refs_3_.refs_0_), custom_call_target="tpu_custom_call" | custom-call | flops 1 | bytes 1 | tf_op jit(solution)/shard_map/op_1/pallas_call | solution.py:144
  26.7 1.7 %collective-permute-done.3.refs_3_ = f32[1024,256]{1,0:T(8,128)S(1)} collective-permute-done((f32[1024,256]{1,0:T(8,128)S(1)}, f32[1024,256]{1,0:T(8,128)S(1)}, u32[]{:S(2)}, u32[]{:S(2)}) %collective-permute-start.3) | collective-permute-done | bytes 1048608 | tf_op jit(solution)/shard_map/ppermute | solution.py:354
  29.2 1.3 %collective-permute-start.8 = (f32[512,256]{1,0:T(8,128)S(1)}, f32[512,256]{1,0:T(8,128)S(1)}, u32[]{:S(2)}, u32[]{:S(2)}) collective-permute-start(f32[512,256]{1,0:T(8,128)S(1)} %o1_2.1.refs_4_), channel_id=1, source_target_pairs={{0,8},{4,36},{8,0},{12,44},{16,24},{20,52},{24,16},{28,60},{32,40}... | collective-permute-start | bytes 1572872 | tf_op jit(solution)/shard_map/ppermute | solution.py:370
  31.2 2.2 %collective-permute-start.9 = (f32[512,256]{1,0:T(8,128)S(1)}, f32[512,256]{1,0:T(8,128)S(1)}, u32[]{:S(2)}, u32[]{:S(2)}) collective-permute-start(f32[512,256]{1,0:T(8,128)S(1)} %o1_3.1.refs_3_), channel_id=1, source_target_pairs={{0,24},{4,100},{8,16},{12,108},{16,8},{20,116},{24,0},{28,124},{32... | collective-permute-start | bytes 1572872 | tf_op jit(solution)/shard_map/ppermute | solution.py:370
  34.9 1.9 %collective-permute-done.5.refs_1_ = f32[512,768]{1,0:T(8,128)S(1)} collective-permute-done((f32[512,768]{1,0:T(8,128)S(1)}, f32[512,768]{1,0:T(8,128)S(1)}, u32[]{:S(2)}, u32[]{:S(2)}) %collective-permute-start.5) | collective-permute-done | bytes 1572896 | tf_op jit(solution)/shard_map/ppermute | solution.py:370
  37.4 2.6 %collective-permute-start.6 = (f32[256,768]{1,0:T(8,128)S(1)}, f32[256,768]{1,0:T(8,128)S(1)}, u32[]{:S(2)}, u32[]{:S(2)}) collective-permute-start(f32[256,768]{1,0:T(8,128)S(1)} %get-tuple-element.39.refs_4_), channel_id=1, source_target_pairs={{0,24},{4,100},{8,16},{12,108},{16,8},{20,116},{24,0},{28,124},{32... | collective-permute-start | bytes 2359304 | tf_op jit(solution)/shard_map/ppermute | solution.py:390
  43.0 2.2 %collective-permute-start.10 = (f32[256,256]{1,0:T(8,128)S(1)}, f32[256,256]{1,0:T(8,128)S(1)}, u32[]{:S(2)}, u32[]{:S(2)}) collective-permute-start(f32[256,256]{1,0:T(8,128)S(1)} %get-tuple-element.42.refs_4_), channel_id=1, source_target_pairs={{0,24},{4,100},{8,16},{12,108},{16,8},{20,116},{24,0},{28,124},{32... | collective-permute-start | bytes 786440 | tf_op jit(solution)/shard_map/ppermute | solution.py:390
  45.2 6.8 %collective-permute-done.12.refs_3_ = f32[256,256]{1,0:T(8,128)S(1)} collective-permute-done((f32[256,256]{1,0:T(8,128)S(1)}, f32[256,256]{1,0:T(8,128)S(1)}, u32[]{:S(2)}, u32[]{:S(2)}) %collective-permute-start.12) | collective-permute-done | bytes 262176 | tf_op jit(solution)/shard_map/ppermute | solution.py:390
  52.1 1.8 %collective-permute-start.14 = (f32[128,1024]{1,0:T(8,128)S(1)}, f32[128,1024]{1,0:T(8,128)S(1)}, u32[]{:S(2)}, u32[]{:S(2)}) collective-permute-start(f32[128,1024]{1,0:T(8,128)S(1)} %get-tuple-element.45.refs_4_), channel_id=1, source_target_pairs={{0,32},{4,12},{8,40},{12,4},{16,48},{20,28},{24,56},{28,20},{32,0}... | collective-permute-start | bytes 1572872 | tf_op jit(solution)/shard_map/ppermute | solution.py:390
  54.1 2.8 %collective-permute-start.13 = (f32[128,1024]{1,0:T(8,128)S(1)}, f32[128,1024]{1,0:T(8,128)S(1)}, u32[]{:S(2)}, u32[]{:S(2)}) collective-permute-start(f32[128,1024]{1,0:T(8,128)S(1)} %get-tuple-element.47.refs_2_), channel_id=1, source_target_pairs={{0,96},{4,28},{8,104},{12,20},{16,112},{20,12},{24,120},{28,4},{32... | collective-permute-start | bytes 1572872 | tf_op jit(solution)/shard_map/ppermute | solution.py:390
  56.9 4.5 %collective-permute-done.14.refs_1_ = f32[128,1024]{1,0:T(8,128)S(1)} collective-permute-done((f32[128,1024]{1,0:T(8,128)S(1)}, f32[128,1024]{1,0:T(8,128)S(1)}, u32[]{:S(2)}, u32[]{:S(2)}) %collective-permute-start.14) | collective-permute-done | bytes 524320 | tf_op jit(solution)/shard_map/ppermute | solution.py:390
  61.4 3.1 %collective-permute-start.16 = (f32[64,1024]{1,0:T(8,128)S(1)}, f32[64,1024]{1,0:T(8,128)S(1)}, u32[]{:S(2)}, u32[]{:S(2)}) collective-permute-start(f32[64,1024]{1,0:T(8,128)S(1)} %get-tuple-element.49.refs_2_), channel_id=1, source_target_pairs={{0,96},{4,28},{8,104},{12,20},{16,112},{20,12},{24,120},{28,4},{32... | collective-permute-start | bytes 786440 | tf_op jit(solution)/shard_map/ppermute | solution.py:390
  64.8 4.3 %collective-permute-done.16.refs_1_ = f32[64,1024]{1,0:T(8,128)S(1)} collective-permute-done((f32[64,1024]{1,0:T(8,128)S(1)}, f32[64,1024]{1,0:T(8,128)S(1)}, u32[]{:S(2)}, u32[]{:S(2)}) %collective-permute-start.16) | collective-permute-done | bytes 262176 | tf_op jit(solution)/shard_map/ppermute | solution.py:390
  69.5 1.6 %collective-permute-done.15.refs_1_ = f32[64,1024]{1,0:T(8,128)S(1)} collective-permute-done((f32[64,1024]{1,0:T(8,128)S(1)}, f32[64,1024]{1,0:T(8,128)S(1)}, u32[]{:S(2)}, u32[]{:S(2)}) %collective-permute-start.15) | collective-permute-done | bytes 262176 | tf_op jit(solution)/shard_map/ppermute | solution.py:390
  71.5 3.9 %collective-permute-start.19 = (f32[8,64]{1,0:T(8,128)S(1)}, f32[8,64]{1,0:T(8,128)S(1)}, u32[]{:S(2)}, u32[]{:S(2)}) collective-permute-start(f32[8,64]{1,0:T(8,128)S(1)} %add.3.refs_0_.refs_4_), channel_id=1, source_target_pairs={{0,2},{1,3},{2,0},{3,1},{4,6},{5,7},{6,4},{7,5},{8,10},{9,11},{10,... | collective-permute-start | bytes 6152 | tf_op jit(solution)/shard_map/ppermute | solution.py:394
  77.4 2.8 %collective-permute-done.18.refs_2_ = f32[8,64]{1,0:T(8,128)S(1)} collective-permute-done((f32[8,64]{1,0:T(8,128)S(1)}, f32[8,64]{1,0:T(8,128)S(1)}, u32[]{:S(2)}, u32[]{:S(2)}) %collective-permute-start.18) | collective-permute-done | bytes 2080 | tf_op jit(solution)/shard_map/ppermute | solution.py:394
  (51 shorter events, 13.8 us)
Async XLA Ops:
  7.2 4.3 %collective-permute-start.1 = (f32[512,768]{1,0:T(8,128)S(1)}, f32[512,768]{1,0:T(8,128)S(1)}, u32[]{:S(2)}, u32[]{:S(2)}) collective-permute-start(f32[512,768]{1,0:T(8,128)S(1)} %get-tuple-element.36.refs_3_), channel_id=1, source_target_pairs={{0,4},{4,0},{8,12},{12,8},{16,20},{20,16},{24,28},{28,24},{32,36},... | collective-permute-start | bytes 4718600 | tf_op jit(solution)/shard_map/ppermute | solution.py:354
  9.0 4.2 %collective-permute-start = (f32[512,768]{1,0:T(8,128)S(1)}, f32[512,768]{1,0:T(8,128)S(1)}, u32[]{:S(2)}, u32[]{:S(2)}) collective-permute-start(f32[512,768]{1,0:T(8,128)S(1)} %s1_1.1.refs_3_), channel_id=1, source_target_pairs={{0,4},{4,0},{8,12},{12,8},{16,20},{20,16},{24,28},{28,24},{32,36},... | collective-permute-start | bytes 4718600 | tf_op jit(solution)/shard_map/ppermute | solution.py:354
  11.6 23.0 %collective-permute-start.2 = (f32[512,768]{1,0:T(8,128)S(1)}, f32[512,768]{1,0:T(8,128)S(1)}, u32[]{:S(2)}, u32[]{:S(2)}) collective-permute-start(f32[512,768]{1,0:T(8,128)S(1)} %a1_0.1.refs_4_), channel_id=1, source_target_pairs={{0,8},{4,36},{8,0},{12,44},{16,24},{20,52},{24,16},{28,60},{32,40}... | collective-permute-start | bytes 4718600 | tf_op jit(solution)/shard_map/ppermute | solution.py:375
  15.1 21.7 %collective-permute-start.5 = (f32[512,768]{1,0:T(8,128)S(1)}, f32[512,768]{1,0:T(8,128)S(1)}, u32[]{:S(2)}, u32[]{:S(2)}) collective-permute-start(f32[512,768]{1,0:T(8,128)S(1)} %o1_1.1.refs_3_), channel_id=1, source_target_pairs={{0,24},{4,100},{8,16},{12,108},{16,8},{20,116},{24,0},{28,124},{32... | collective-permute-start | bytes 4718600 | tf_op jit(solution)/shard_map/ppermute | solution.py:370
  21.0 15.9 %collective-permute-start.4 = (f32[1024,768]{1,0:T(8,128)S(1)}, f32[1024,768]{1,0:T(8,128)S(1)}, u32[]{:S(2)}, u32[]{:S(2)}) collective-permute-start(f32[1024,768]{1,0:T(8,128)S(1)} %s0_01.1.refs_3_), channel_id=1, source_target_pairs={{0,4},{4,0},{8,12},{12,8},{16,20},{20,16},{24,28},{28,24},{32,36},... | collective-permute-start | bytes 9437192 | tf_op jit(solution)/shard_map/ppermute | solution.py:354
  22.7 5.8 %collective-permute-start.3 = (f32[1024,256]{1,0:T(8,128)S(1)}, f32[1024,256]{1,0:T(8,128)S(1)}, u32[]{:S(2)}, u32[]{:S(2)}) collective-permute-start(f32[1024,256]{1,0:T(8,128)S(1)} %s1_23.1.refs_3_), channel_id=1, source_target_pairs={{0,4},{4,0},{8,12},{12,8},{16,20},{20,16},{24,28},{28,24},{32,36},... | collective-permute-start | bytes 3145736 | tf_op jit(solution)/shard_map/ppermute | solution.py:354
  29.2 13.8 %collective-permute-start.8 = (f32[512,256]{1,0:T(8,128)S(1)}, f32[512,256]{1,0:T(8,128)S(1)}, u32[]{:S(2)}, u32[]{:S(2)}) collective-permute-start(f32[512,256]{1,0:T(8,128)S(1)} %o1_2.1.refs_4_), channel_id=1, source_target_pairs={{0,8},{4,36},{8,0},{12,44},{16,24},{20,52},{24,16},{28,60},{32,40}... | collective-permute-start | bytes 1572872 | tf_op jit(solution)/shard_map/ppermute | solution.py:370
  31.2 11.2 %collective-permute-start.9 = (f32[512,256]{1,0:T(8,128)S(1)}, f32[512,256]{1,0:T(8,128)S(1)}, u32[]{:S(2)}, u32[]{:S(2)}) collective-permute-start(f32[512,256]{1,0:T(8,128)S(1)} %o1_3.1.refs_3_), channel_id=1, source_target_pairs={{0,24},{4,100},{8,16},{12,108},{16,8},{20,116},{24,0},{28,124},{32... | collective-permute-start | bytes 1572872 | tf_op jit(solution)/shard_map/ppermute | solution.py:370
  34.6 5.3 %collective-permute-start.7 = (f32[1024,256]{1,0:T(8,128)S(1)}, f32[1024,256]{1,0:T(8,128)S(1)}, u32[]{:S(2)}, u32[]{:S(2)}) collective-permute-start(f32[1024,256]{1,0:T(8,128)S(1)} %s0_23.1.refs_2_), channel_id=1, source_target_pairs={{0,4},{4,0},{8,12},{12,8},{16,20},{20,16},{24,28},{28,24},{32,36},... | collective-permute-start | bytes 3145736 | tf_op jit(solution)/shard_map/ppermute | solution.py:354
  37.1 14.9 %collective-permute-start.11 = (f32[256,768]{1,0:T(8,128)S(1)}, f32[256,768]{1,0:T(8,128)S(1)}, u32[]{:S(2)}, u32[]{:S(2)}) collective-permute-start(f32[256,768]{1,0:T(8,128)S(1)} %get-tuple-element.37.refs_2_), channel_id=1, source_target_pairs={{0,8},{4,36},{8,0},{12,44},{16,24},{20,52},{24,16},{28,60},{32,40}... | collective-permute-start | bytes 2359304 | tf_op jit(solution)/shard_map/ppermute | solution.py:390
  37.4 16.6 %collective-permute-start.6 = (f32[256,768]{1,0:T(8,128)S(1)}, f32[256,768]{1,0:T(8,128)S(1)}, u32[]{:S(2)}, u32[]{:S(2)}) collective-permute-start(f32[256,768]{1,0:T(8,128)S(1)} %get-tuple-element.39.refs_4_), channel_id=1, source_target_pairs={{0,24},{4,100},{8,16},{12,108},{16,8},{20,116},{24,0},{28,124},{32... | collective-permute-start | bytes 2359304 | tf_op jit(solution)/shard_map/ppermute | solution.py:390
  42.4 9.5 %collective-permute-start.12 = (f32[256,256]{1,0:T(8,128)S(1)}, f32[256,256]{1,0:T(8,128)S(1)}, u32[]{:S(2)}, u32[]{:S(2)}) collective-permute-start(f32[256,256]{1,0:T(8,128)S(1)} %get-tuple-element.40.refs_2_), channel_id=1, source_target_pairs={{0,8},{4,36},{8,0},{12,44},{16,24},{20,52},{24,16},{28,60},{32,40}... | collective-permute-start | bytes 786440 | tf_op jit(solution)/shard_map/ppermute | solution.py:390
  43.0 11.0 %collective-permute-start.10 = (f32[256,256]{1,0:T(8,128)S(1)}, f32[256,256]{1,0:T(8,128)S(1)}, u32[]{:S(2)}, u32[]{:S(2)}) collective-permute-start(f32[256,256]{1,0:T(8,128)S(1)} %get-tuple-element.42.refs_4_), channel_id=1, source_target_pairs={{0,24},{4,100},{8,16},{12,108},{16,8},{20,116},{24,0},{28,124},{32... | collective-permute-start | bytes 786440 | tf_op jit(solution)/shard_map/ppermute | solution.py:390
  52.1 9.3 %collective-permute-start.14 = (f32[128,1024]{1,0:T(8,128)S(1)}, f32[128,1024]{1,0:T(8,128)S(1)}, u32[]{:S(2)}, u32[]{:S(2)}) collective-permute-start(f32[128,1024]{1,0:T(8,128)S(1)} %get-tuple-element.45.refs_4_), channel_id=1, source_target_pairs={{0,32},{4,12},{8,40},{12,4},{16,48},{20,28},{24,56},{28,20},{32,0}... | collective-permute-start | bytes 1572872 | tf_op jit(solution)/shard_map/ppermute | solution.py:390
  54.1 15.0 %copy-start = (f32[64,2048]{1,0:T(8,128)S(1)}, f32[64,2048]{1,0:T(8,128)}, u32[]{:S(2)}) copy-start(f32[64,2048]{1,0:T(8,128)} %refs_2_.3) | copy-start | bytes 1572868
  54.1 15.0 %copy-start.1 = (f32[64,2048]{1,0:T(8,128)S(1)}, f32[64,2048]{1,0:T(8,128)}, u32[]{:S(2)}) copy-start(f32[64,2048]{1,0:T(8,128)} %refs_3_.3) | copy-start | bytes 1572868
  54.1 15.0 %copy-start.2 = (f32[64,2048]{1,0:T(8,128)S(1)}, f32[64,2048]{1,0:T(8,128)}, u32[]{:S(2)}) copy-start(f32[64,2048]{1,0:T(8,128)} %refs_4_.3) | copy-start | bytes 1572868
  54.1 10.5 %collective-permute-start.13 = (f32[128,1024]{1,0:T(8,128)S(1)}, f32[128,1024]{1,0:T(8,128)S(1)}, u32[]{:S(2)}, u32[]{:S(2)}) collective-permute-start(f32[128,1024]{1,0:T(8,128)S(1)} %get-tuple-element.47.refs_2_), channel_id=1, source_target_pairs={{0,96},{4,28},{8,104},{12,20},{16,112},{20,12},{24,120},{28,4},{32... | collective-permute-start | bytes 1572872 | tf_op jit(solution)/shard_map/ppermute | solution.py:390
  61.4 7.7 %collective-permute-start.16 = (f32[64,1024]{1,0:T(8,128)S(1)}, f32[64,1024]{1,0:T(8,128)S(1)}, u32[]{:S(2)}, u32[]{:S(2)}) collective-permute-start(f32[64,1024]{1,0:T(8,128)S(1)} %get-tuple-element.49.refs_2_), channel_id=1, source_target_pairs={{0,96},{4,28},{8,104},{12,20},{16,112},{20,12},{24,120},{28,4},{32... | collective-permute-start | bytes 786440 | tf_op jit(solution)/shard_map/ppermute | solution.py:390
  64.6 6.5 %collective-permute-start.15 = (f32[64,1024]{1,0:T(8,128)S(1)}, f32[64,1024]{1,0:T(8,128)S(1)}, u32[]{:S(2)}, u32[]{:S(2)}) collective-permute-start(f32[64,1024]{1,0:T(8,128)S(1)} %get-tuple-element.51.refs_5_), channel_id=1, source_target_pairs={{0,32},{4,12},{8,40},{12,4},{16,48},{20,28},{24,56},{28,20},{32,0}... | collective-permute-start | bytes 786440 | tf_op jit(solution)/shard_map/ppermute | solution.py:390
  71.5 5.9 %collective-permute-start.19 = (f32[8,64]{1,0:T(8,128)S(1)}, f32[8,64]{1,0:T(8,128)S(1)}, u32[]{:S(2)}, u32[]{:S(2)}) collective-permute-start(f32[8,64]{1,0:T(8,128)S(1)} %add.3.refs_0_.refs_4_), channel_id=1, source_target_pairs={{0,2},{1,3},{2,0},{3,1},{4,6},{5,7},{6,4},{7,5},{8,10},{9,11},{10,... | collective-permute-start | bytes 6152 | tf_op jit(solution)/shard_map/ppermute | solution.py:394
  75.4 4.8 %collective-permute-start.18 = (f32[8,64]{1,0:T(8,128)S(1)}, f32[8,64]{1,0:T(8,128)S(1)}, u32[]{:S(2)}, u32[]{:S(2)}) collective-permute-start(f32[8,64]{1,0:T(8,128)S(1)} %add.3.refs_0_.refs_4_), channel_id=1, source_target_pairs={{0,3},{1,2},{2,1},{3,0},{4,7},{5,6},{6,5},{7,4},{8,11},{9,10},{10,... | collective-permute-start | bytes 6152 | tf_op jit(solution)/shard_map/ppermute | solution.py:394
  76.1 4.1 %collective-permute-start.17 = (f32[8,64]{1,0:T(8,128)S(1)}, f32[8,64]{1,0:T(8,128)S(1)}, u32[]{:S(2)}, u32[]{:S(2)}) collective-permute-start(f32[8,64]{1,0:T(8,128)S(1)} %add.3.refs_0_.refs_4_), channel_id=1, source_target_pairs={{0,1},{1,0},{2,3},{3,2},{4,5},{5,4},{6,7},{7,6},{8,9},{9,8},{10,11... | collective-permute-start | bytes 6152 | tf_op jit(solution)/shard_map/ppermute | solution.py:394
